TPU v7x, 256 devices: a whole 4x4x8 slice. The times are simulated.
256 devices in a mesh: freq: 8 (over x, y_hi), space: 32 (over z, y_lo, core).
Axes of the slice: x: 4, y: 4 (y_hi: 2, y_lo: 2; y = y_hi * 2 + y_lo), z: 8, core: 2. Of those that a mesh axis runs over, the one named last changes fastest.
Arguments:
- source_current: float32 [8, 2, 2, 3, 128, 16, 256], P('freq', None, None, None, 'space'), may hold values from -60 to 60
- conductivity: float32 [128, 16, 256], P('space', None, 'freq'), may hold values from 1 to 10
- frequency: float32 [8], P('freq'), may hold values from 4 to 16
- station_cells: int32 [2048], P('space'), may hold values from 0 to 1023
- station_depth: int32 [2048], P('space'), may hold values from 0 to 15
Outputs:
- electric_field: float32 [8, 2, 2, 3, 128, 16, 256], P('freq', None, None, None, 'space')
- predicted: float32 [8, 2, 2, 3, 2048], P('freq', None, None, None, 'space')
- gradient: float32 [128, 16, 256], P('space', None, 'freq')
Inputs may be any that keep to these rules, and one draw needn't show every extreme that they name: `station_cells`: A station's cell lies in the tile of the devices that hold the station. `station_depth`: depth index of a station's cell.
All inputs are finite; a program needn't handle non-finite values.
Results may differ from a plain program's by a relative error of at most 0.00026.
Values sent between devices are 32-bit elements; how exact they have to be, the bound alone decides.
No kernel may reach another device: no remote copies, remote signals or barrier semaphores. Data moves between devices by JAX's collectives and lax.ppermute only.
A program may use at most 64 MiB of HBM per device.

v0:
```python
import jax
import jax.numpy as jnp
from jax import lax
from jax.sharding import PartitionSpec as P

ITERS = 2


def with_halo(cells, sides, width):
    for axis, dim in sides:
        count = lax.axis_size(axis)
        ends = count - 1
        head = lax.slice_in_dim(cells, 0, width, axis=dim)
        tail = lax.slice_in_dim(cells, cells.shape[dim] - width, cells.shape[dim], axis=dim)
        cells = jnp.concatenate(
            [
                lax.ppermute(tail, axis, [(i, (i + 1) % count) for i in range(ends)]),
                cells,
                lax.ppermute(head, axis, [((i + 1) % count, i) for i in range(ends)]),
            ],
            axis=dim,
        )
    return cells


def forward_x(array_in):
    return array_in[..., 1:, :-1, :-1] - array_in[..., :-1, :-1, :-1]


def forward_z(array_in):
    return array_in[..., :, 1:, :-1] - array_in[..., :, :-1, :-1]


def forward_y(array_in):
    return array_in[..., :, :-1, 1:] - array_in[..., :, :-1, :-1]


def backward_x(array_in):
    return array_in[..., 1:, 1:, 1:] - array_in[..., :-1, 1:, 1:]


def backward_z(array_in):
    return array_in[..., :, 1:, 1:] - array_in[..., :, :-1, 1:]


def backward_y(array_in):
    return array_in[..., :, 1:, 1:] - array_in[..., :, 1:, :-1]


def magnetic(edge_x, edge_y, edge_z):
    inner_y = edge_y[..., :-1, :, :]
    inner_z = edge_z[..., :-1, :, :]
    face_x = forward_y(inner_z) - forward_z(inner_y)
    face_y = forward_z(edge_x) - forward_x(edge_z)
    face_z = forward_x(edge_y) - forward_y(edge_x)
    return (face_x, face_y, face_z)


def curl_back(face_x, face_y, face_z):
    trim_y = face_y[..., 1:, :, :]
    trim_z = face_z[..., 1:, :, :]
    curl_x = backward_y(trim_z) - backward_z(trim_y)
    curl_y = backward_z(face_x) - backward_x(face_z)
    curl_z = backward_x(face_y) - backward_y(face_x)
    return jnp.stack([curl_x, curl_y, curl_z], axis=-4)


def curl_padded(padded):
    faces = magnetic(padded[..., 0, :-1, :, :], padded[..., 1, :, :, :], padded[..., 2, :, :, :])
    return curl_back(faces[0][..., 1:, :, :], faces[1], faces[2])


def curl_local(stacked):
    plane_pad = [(0, 0)] * 5 + [(1, 1), (1, 1)]
    padded = with_halo(stacked, (("space", 4),), 1)
    return curl_padded(jnp.pad(padded, plane_pad))


def inner_product(left, right):
    real = jnp.sum(left[:, 0] * right[:, 0] + left[:, 1] * right[:, 1], axis=(1, 2, 3, 4))
    imag = jnp.sum(left[:, 0] * right[:, 1] - left[:, 1] * right[:, 0], axis=(1, 2, 3, 4))
    return jnp.stack([real, imag])


def divide_complex(left, right):
    denom = right[0] * right[0] + right[1] * right[1]
    return jnp.stack(
        [
            (left[0] * right[0] + left[1] * right[1]) / denom,
            (left[1] * right[0] - left[0] * right[1]) / denom,
        ]
    )


def conjugate(value):
    return jnp.stack([value[0], -value[1]])


def scale_field(factor, electric):
    real_part = factor[0][:, None, None, None, None]
    imag_part = factor[1][:, None, None, None, None]
    return jnp.stack(
        [
            real_part * electric[:, 0] - imag_part * electric[:, 1],
            real_part * electric[:, 1] + imag_part * electric[:, 0],
        ],
        axis=1,
    )


def residual_product(shadow_res, residual):
    return lax.psum(inner_product(shadow_res, residual), "space")


def local(source_current, conductivity, frequency, station_cells, station_depth):
    whole_sigma = lax.all_gather(conductivity, "freq", axis=2, tiled=True)
    damping = frequency[0] * whole_sigma
    rhs = source_current[0]
    orient = jnp.array([1.0, -1.0], jnp.float32).reshape(2, 1, 1, 1, 1, 1)
    solution = jnp.zeros_like(rhs)
    adjoint = jnp.zeros_like(rhs)
    residual = rhs
    shadow_res = rhs
    direction = rhs
    shadow_dir = rhs
    rho_now = residual_product(shadow_res, residual)
    for step in range(ITERS):
        stacked = jnp.stack([direction, shadow_dir])
        curl = curl_local(stacked)
        real = curl[:, :, 0] - orient * damping * stacked[:, :, 1]
        imag = curl[:, :, 1] + orient * damping * stacked[:, :, 0]
        result = jnp.stack([real, imag], axis=2)
        image = result[0]
        shadow_img = result[1]
        curvature = lax.psum(inner_product(shadow_dir, image), "space")
        step_size = divide_complex(rho_now, curvature)
        solution = solution + scale_field(step_size, direction)
        residual = residual - scale_field(step_size, image)
        adjoint = adjoint + scale_field(conjugate(step_size), shadow_dir)
        shadow_res = shadow_res - scale_field(conjugate(step_size), shadow_img)
        if step + 1 < ITERS:
            rho_next = residual_product(shadow_res, residual)
            ratio_next = divide_complex(rho_next, rho_now)
            direction = residual + scale_field(ratio_next, direction)
            shadow_dir = shadow_res + scale_field(conjugate(ratio_next), shadow_dir)
            rho_now = rho_next
    width_y = rhs.shape[-1]
    depth_cells = rhs.shape[-2]
    pols_here = rhs.shape[0]
    flat_index = (
        station_cells // width_y * depth_cells + station_depth
    ) * width_y + station_cells % width_y
    sampled = jnp.take(solution.reshape(pols_here * 6, -1), flat_index, axis=1).reshape(
        1, pols_here, 2, 3, -1
    )
    sensitivity = frequency[0] * jnp.sum(
        adjoint[:, 0] * solution[:, 0] - adjoint[:, 1] * solution[:, 1], axis=(0, 1)
    )
    summed = lax.psum_scatter(sensitivity, "freq", scatter_dimension=2, tiled=True)
    gradient = conductivity * summed / (3.0 * pols_here * lax.axis_size("freq"))
    return (solution[None], sampled, gradient)


def solution(mesh):
    return jax.shard_map(
        local,
        mesh=mesh,
        in_specs=(
            P("freq", None, None, None, "space", None, None),
            P("space", None, "freq"),
            P("freq"),
            P("space"),
            P("space"),
        ),
        out_specs=(
            P("freq", None, None, None, "space", None, None),
            P("freq", None, None, None, "space"),
            P("space", None, "freq"),
        ),
        check_vma=False,
    )
```

profile of v0, /device:TPU:1, one launch (start us, length us, event | category | flops | bytes accessed | tf_op | source)
XLA Modules:
  0.0 334.7 jit_solution(12438344875053515600)
XLA Ops:
  7.2 1.3 fusion.55
  8.6 4.6 %collective-permute-start = (f32[2,2,2,3,1,16,256]{6,5,4,3,1,2,0:T(8,128)S(1)}, f32[2,2,2,3,1,16,256]{6,5,4,3,1,2,0:T(8,128)S(1)}, u32[]{:S(2)}, u32[]{:S(2)}) collective-permute-start(f32[2,2,2,3,1,16,256]{6,5,4,3,1,2,0:T(8,128)S(1)} %get-tuple-element.50), channel_id=1, source_target_pairs={{0,1},{1,2},{2,3},{3,4},{4,5},{5,6},{6,7},{7,8},{8,9},{9,10},{10,1... | collective-permute-start | bytes 1179656 | tf_op jit(solution)/shard_map/ppermute | solution.py:17
  13.2 1.9 collective-permute-start.1
  15.8 0.1 copy.75
  15.9 33.6 %all_gather.3 = f32[4,16,256]{1,0,2:T(4,128)S(1)} all-gather(f32[4,16,32]{1,0,2:T(4,128)S(1)} %copy.75), channel_id=1, replica_groups=mesh['freq'=8,'space'=32] {'freq'}, dimensions={2}, use_global_device_ids=true | all-gather | bytes 73728 | tf_op jit(solution)/shard_map/all_gather | solution.py:116
  49.5 0.2 copy.76
  49.9 2.4 select_maximum_fusion.2
  52.3 0.1 slice_bitcast_fusion.5
  52.4 0.3 slice_bitcast_fusion.2
  52.7 0.9 fusion.11
  53.6 1.1 fusion.37
  54.7 0.2 pad_maximum_fusion.2
  54.9 0.2 fusion.54
  55.1 0.3 fusion.22
  55.4 0.3 fusion.21
  55.6 0.4 add_reduce_fusion.2
  56.1 60.6 %all-reduce.2 = (f32[2,2]{1,0:T(2,128)S(1)}, f32[2,2]{1,0:T(2,128)S(1)}) all-reduce(f32[2,2]{1,0:T(2,128)S(1)} %pad_maximum_fusion.8, f32[2,2]{1,0:T(2,128)S(1)} %pad_maximum_fusion.7), channel_id=1, replica_groups=mesh['freq'=8,'space'=32] {'space'}, use_global_device_ids=true, to_apply=%region_5.6 | all-reduce | flops 8 | bytes 64 | tf_op jit(solution)/shard_map/psum | solution.py:135
  116.7 1.3 multiply_subtract_fusion.1
  118.1 0.3 maximum_subtract_fusion
  118.3 0.5 copy-done.2
  118.8 0.1 copy-done.4
  118.9 0.1 copy-done.6
  119.1 0.1 copy-done.8
  119.2 0.3 add_reduce_fusion.1
  119.6 52.5 %psum.30 = f32[2,2]{1,0:T(2,128)S(1)} all-reduce(f32[2,2]{1,0:T(2,128)S(1)} %pad_maximum_fusion.9), channel_id=1, replica_groups=mesh['freq'=8,'space'=32] {'space'}, use_global_device_ids=true, to_apply=%region_8.9 | all-reduce | flops 4 | bytes 32 | tf_op jit(solution)/shard_map/psum | solution.py:112
  172.1 0.3 multiply_subtract_fusion.4
  172.4 0.7 copy-done.3
  173.1 0.1 copy-done.5
  173.2 0.1 copy-done.7
  173.3 0.1 copy-done.9
  173.4 0.5 fusion.25
  174.0 1.9 collective-permute-start.2
  175.9 2.4 collective-permute-start.3
  178.4 0.1 maximum_add_fusion
  178.6 6.3 %collective-permute-done.2 = f32[2,2,2,3,1,16,256]{6,5,4,1,2,0,3:T(8,128)S(1)} collective-permute-done((f32[2,2,2,3,1,16,256]{6,5,4,1,2,0,3:T(8,128)S(1)}, f32[2,2,2,3,1,16,256]{6,5,4,1,2,0,3:T(8,128)S(1)}, u32[]{:S(2)}, u32[]{:S(2)}) %collective-permute-start.2) | collective-permute-done | bytes 393248 | tf_op jit(solution)/shard_map/ppermute | solution.py:17
  184.9 0.2 collective-permute-done.3
  185.0 2.4 select_maximum_fusion
  187.5 0.1 slice_bitcast_fusion.4
  187.6 0.2 slice_bitcast_fusion
  187.8 0.9 fusion.8
  188.7 1.1 fusion.31
  189.8 0.2 pad_maximum_fusion.3
  189.9 0.7 copy-done.13
  190.7 0.4 fusion.16
  191.2 0.3 add_reduce_fusion
  191.5 0.1 maximum_add_fusion.1
  191.6 50.7 %psum.31 = f32[2,2]{1,0:T(2,128)S(1)} all-reduce(f32[2,2]{1,0:T(2,128)S(1)} %pad_maximum_fusion.10), channel_id=1, replica_groups=mesh['freq'=8,'space'=32] {'space'}, use_global_device_ids=true, to_apply=%region_11.12 | all-reduce | flops 4 | bytes 32 | tf_op jit(solution)/shard_map/psum | solution.py:135
  242.3 0.3 multiply_subtract_fusion
  242.6 0.7 copy-done.1
  243.3 0.2 maximum_add_fusion.3
  243.6 0.7 copy-done.10
  244.3 0.1 copy-done.11
  244.5 0.1 maximum_add_fusion.4
  244.6 0.2 fusion.39
  244.8 0.2 add.217
  245.0 0.2 copy.92
  245.2 0.9 reshape.381
  246.1 4.6 %copy.89 = f32[12,16384]{0,1:T(8,128)} copy(f32[12,16384]{1,0:T(8,128)S(1)} %add.217) | data formatting | bytes 1572864 | tf_op jit(solution)/shard_map/add | solution.py:137
  250.8 4.0 %gather_fusion = f32[64,12]{1,0:T(8,128)S(1)} fusion(f32[12,16384]{0,1:T(8,128)} %copy.89, s32[1024]{0:T(1024)S(1)} %pad_clamp_fusion), kind=kCustom, calls=%fused_computation | custom fusion | bytes 6400 | tf_op jit(solution)/shard_map/jit(_take)/gather | solution.py:153
  254.9 0.6 copy.91
  255.5 1.1 maximum_add_fusion.2
  256.5 69.8 %reduce-scatter.4.cloned.1.call-done = f32[32,64]{1,0:T(8,128)} async-done(((f32[256,64]{1,0:T(8,128)}), f32[32,64]{1,0:T(8,128)}) %reduce-scatter.4.cloned.1.call-update) | async-done | bytes 8208
  326.3 0.8 reshape.382
  327.2 0.6 multiply_multiply_fusion
  (52 shorter events, 0.7 us)
Async XLA Ops:
  7.2 42.6 %copy-start.16 = (f32[2]{0:T(128)S(1)}, f32[2]{0:T(128)}, u32[]{:S(2)}) copy-start(f32[2]{0:T(128)} %constant.55.clone) | copy-start | bytes 28
  7.2 42.7 %copy-start = (f32[1,2,2,3,4,16,256]{6,5,4,3,2,1,0:T(8,128)S(1)}, f32[1,2,2,3,4,16,256]{6,5,4,3,2,1,0:T(8,128)}, u32[]{:S(2)}) copy-start(f32[1,2,2,3,4,16,256]{6,5,4,3,2,1,0:T(8,128)} %param.6) | copy-start | bytes 2359300
  7.2 8.6 %copy-start.14 = (f32[4,16,32]{2,1,0:T(8,128)S(1)}, f32[4,16,32]{2,1,0:T(8,128)}, u32[]{:S(2)}) copy-start(f32[4,16,32]{2,1,0:T(8,128)} %param.7) | copy-start | bytes 24580
  7.2 319.1 %reduce-scatter.4.cloned.1.call-start = ((), (), s32[]{:S(2)}) async-start(), calls=%async_computation.1 | async-start | bytes 147456
  8.6 41.2 %collective-permute-start = (f32[2,2,2,3,1,16,256]{6,5,4,3,1,2,0:T(8,128)S(1)}, f32[2,2,2,3,1,16,256]{6,5,4,3,1,2,0:T(8,128)S(1)}, u32[]{:S(2)}, u32[]{:S(2)}) collective-permute-start(f32[2,2,2,3,1,16,256]{6,5,4,3,1,2,0:T(8,128)S(1)} %get-tuple-element.50), channel_id=1, source_target_pairs={{0,1},{1,2},{2,3},{3,4},{4,5},{5,6},{6,7},{7,8},{8,9},{9,10},{10,1... | collective-permute-start | bytes 1179656 | tf_op jit(solution)/shard_map/ppermute | solution.py:17
  13.2 36.6 %collective-permute-start.1 = (f32[2,2,2,3,1,16,256]{6,5,4,3,1,2,0:T(8,128)S(1)}, f32[2,2,2,3,1,16,256]{6,5,4,3,1,2,0:T(8,128)S(1)}, u32[]{:S(2)}, u32[]{:S(2)}) collective-permute-start(f32[2,2,2,3,1,16,256]{6,5,4,3,1,2,0:T(8,128)S(1)} %get-tuple-element.51), channel_id=1, source_target_pairs={{1,0},{2,1},{3,2},{4,3},{5,4},{6,5},{7,6},{8,7},{9,8},{10,9},{11,1... | collective-permute-start | bytes 1179656 | tf_op jit(solution)/shard_map/ppermute | solution.py:19
  49.8 5.2 %copy-start.12 = (f32[2,4,16,256]{3,2,1,0:T(8,128)}, f32[2,4,16,256]{3,2,1,0:T(8,128)S(1)}, u32[]{:S(2)}) copy-start(f32[2,4,16,256]{3,2,1,0:T(8,128)S(1)} %broadcast_multiply_fusion) | copy-start | bytes 393220
  118.1 0.7 copy-start.2
  118.1 0.9 copy-start.4
  118.1 1.0 copy-start.6
  118.1 1.2 copy-start.8
  172.1 1.0 copy-start.3
  172.1 1.1 copy-start.5
  172.1 1.2 copy-start.7
  172.1 1.3 copy-start.9
  173.9 4.5 %copy-start.17 = (s32[64]{0:T(128)S(1)}, s32[64]{0:T(128)}, u32[]{:S(2)}) copy-start(s32[64]{0:T(128)} %param.10) | copy-start | bytes 772
  173.9 4.5 %copy-start.18 = (s32[64]{0:T(128)S(1)}, s32[64]{0:T(128)}, u32[]{:S(2)}) copy-start(s32[64]{0:T(128)} %param.9) | copy-start | bytes 772
  174.0 10.8 %collective-permute-start.2 = (f32[2,2,2,3,1,16,256]{6,5,4,1,2,0,3:T(8,128)S(1)}, f32[2,2,2,3,1,16,256]{6,5,4,1,2,0,3:T(8,128)S(1)}, u32[]{:S(2)}, u32[]{:S(2)}) collective-permute-start(f32[2,2,2,3,1,16,256]{6,5,4,1,2,0,3:T(8,128)S(1)} %get-tuple-element.44), channel_id=1, source_target_pairs={{0,1},{1,2},{2,3},{3,4},{4,5},{5,6},{6,7},{7,8},{8,9},{9,10},{10,1... | collective-permute-start | bytes 1179656 | tf_op jit(solution)/shard_map/ppermute | solution.py:17
  175.9 9.1 %collective-permute-start.3 = (f32[2,2,2,3,1,16,256]{6,5,4,1,2,0,3:T(8,128)S(1)}, f32[2,2,2,3,1,16,256]{6,5,4,1,2,0,3:T(8,128)S(1)}, u32[]{:S(2)}, u32[]{:S(2)}) collective-permute-start(f32[2,2,2,3,1,16,256]{6,5,4,1,2,0,3:T(8,128)S(1)} %get-tuple-element.45), channel_id=1, source_target_pairs={{1,0},{2,1},{3,2},{4,3},{5,4},{6,5},{7,6},{8,7},{9,8},{10,9},{11,1... | collective-permute-start | bytes 1179656 | tf_op jit(solution)/shard_map/ppermute | solution.py:19
  189.8 0.9 copy-start.13
  242.3 1.0 copy-start.1
  243.3 1.0 copy-start.10
  243.3 1.1 copy-start.11
  250.8 76.4 %copy-start.15 = (f32[4,16,32]{2,1,0:T(8,128)S(1)}, f32[4,16,32]{2,1,0:T(8,128)}, u32[]{:S(2)}) copy-start(f32[4,16,32]{2,1,0:T(8,128)} %param.7) | copy-start | bytes 24580
Sparse Core Ops, SparseCore 0:
  246.3 80.0 reduce-scatter.3
where the time goes:
time: 336 us; the launch traced here: 335 us
  blocking collectives  197 us (59%)
  waiting for transfers between devices  76.3 us (23%)
  other arithmetic  18 us (5%)
  local copies, waits for them, and re-layouts  17 us (5%)
  between operations  15.1 us (4%)
  starting transfers between devices  10.9 us (3%)
    psum x2, blocking collectives, local(): curvature = lax.psum(inner_product(shadow_dir, image), 'space')  111 us
    unnamed x2, waiting for transfers between devices  69.8 us
    psum x1, blocking collectives, residual_product(): return lax.psum(inner_product(shadow_res, residual), 'space')  52.5 us
    all_gather x1, blocking collectives, local(): whole_sigma = lax.all_gather(conductivity, 'freq', axis=2, tiled=True)  33.6 us
    unnamed x44, local copies, waits for them, and re-layouts  6.95 us
  transfers between devices with their start and end apart: 5, of which 3 were waited for; matrix products, arithmetic and copies ran while one was open for 3% of the time, Pallas kernels for 0%

commit v1 on v0

v1 whole, which is shorter than its diff:
```python
import functools
import jax
import jax.numpy as jnp
from jax import lax
from jax.experimental import pallas as pl
from jax.experimental.pallas import tpu as pltpu
from jax.sharding import PartitionSpec as P

F32 = jnp.float32
N_FREQ = 8
N_SPACE = 32
DEPTH = 16
WIDTH = 256
PLANES = 4
SLAB = WIDTH // N_FREQ
LIMIT = 24 * 1024 * 1024


def params():
    return pltpu.CompilerParams(vmem_limit_bytes=LIMIT)


def vmem():
    return pl.BlockSpec(memory_space=pltpu.VMEM)


def anywhere():
    return pl.BlockSpec(memory_space=pl.ANY)


def smem():
    return pl.BlockSpec(memory_space=pltpu.SMEM)


def iota(dim, shape=(DEPTH, WIDTH)):
    return lax.broadcasted_iota(jnp.int32, shape, dim)


class Stencil:
    def __init__(self):
        row, lane = iota(0), iota(1)
        self.first_row, self.last_row = row == 0, row == DEPTH - 1
        self.first_lane, self.last_lane = lane == 0, lane == WIDTH - 1

    def fy(self, f):
        return jnp.where(self.last_lane, 0.0, pltpu.roll(f, WIDTH - 1, 1)) - f

    def fz(self, f):
        return jnp.where(self.last_row, 0.0, pltpu.roll(f, DEPTH - 1, 0)) - f

    def by(self, g, before):
        return g - jnp.where(self.first_lane, before, pltpu.roll(g, 1, 1))

    def bz(self, g, before):
        return g - jnp.where(self.first_row, before, pltpu.roll(g, 1, 0))

    def faces_yz(self, ex, ey, ez, ey_next, ez_next):
        return self.fz(ex) - (ez_next - ez), (ey_next - ey) - self.fy(ex)

    def face_x(self, ey, ez):
        return self.fy(ez) - self.fz(ey)

    def edge_terms(self, px, py, pz):
        return jnp.where(self.first_lane, px + pz, 0.0) + jnp.where(self.first_row, px + py, 0.0)


def fold(plane):
    half = plane[:8] + plane[8:]
    return half[:, :128] + half[:, 128:]


def dot3(a, b):
    return a[0] * b[0] + a[1] * b[1] + a[2] * b[2]


def send_kernel(b_ref, right_ref, left_ref, sems):
    copies = [
        pltpu.make_async_copy(b_ref.at[:, :, :, 0], right_ref.at[:, :, pl.ds(0, 3)], sems.at[0]),
        pltpu.make_async_copy(b_ref.at[:, :, pl.ds(1, 2), 1], right_ref.at[:, :, pl.ds(3, 2)], sems.at[1]),
        pltpu.make_async_copy(b_ref.at[:, :, :, PLANES - 1], left_ref, sems.at[2]),
    ]
    for copy in copies:
        copy.start()
    for copy in copies:
        copy.wait()


def pack_kernel(own_ref, next_ref, out_ref):
    own = jnp.concatenate([own_ref[i] for i in range(PLANES)], axis=1)
    after = jnp.concatenate([next_ref[0]] * PLANES, axis=1)
    for f in range(N_FREQ):
        out_ref[f, 0] = own
        out_ref[f, 1] = after


def curl_kernel(b_ref, low_ref, high_ref, u_ref, unext_ref, face_ref, t_ref, acc_ref):
    st = Stencil()
    place = lax.axis_index("space")
    keep_next = jnp.where(place == N_SPACE - 1, 0.0, 1.0).astype(F32)
    is_first = jnp.where(place == 0, 1.0, 0.0).astype(F32)

    def one_pol(pol, carry):
        s0 = jnp.zeros((8, 128), F32)
        s1 = jnp.zeros((8, 128), F32)
        s2 = jnp.zeros((8, 128), F32)
        s3 = jnp.zeros((8, 128), F32)
        for part in range(2):
            def field(c, i):
                if i < 0:
                    return low_ref[pol, part, c]
                if i < PLANES:
                    return b_ref[pol, part, c, i]
                if i == PLANES:
                    return high_ref[pol, part, c]
                return high_ref[pol, part, c + 2]

            hy_old, hz_old = st.faces_yz(field(0, -1), field(1, -1), field(2, -1), field(1, 0), field(2, 0))
            u_old = None
            for i in range(PLANES + 1):
                ex, ey, ez = field(0, i), field(1, i), field(2, i)
                hx = st.face_x(ey, ez)
                hy, hz = st.faces_yz(ex, ey, ez, field(1, i + 1), field(2, i + 1))
                uy = st.bz(hx, -ey) - (hz - hz_old)
                uz = (hy - hy_old) - st.by(hx, ez)
                hy_old, hz_old = hy, hz
                if i < PLANES:
                    ux = st.by(hz, -ex) - st.bz(hy, ex)
                    u_ref[pol, part, 0, i] = ux
                    u_ref[pol, part, 1, i] = uy
                    u_ref[pol, part, 2, i] = uz
                    s0 = s0 + fold(ex * ex + ey * ey + ez * ez)
                    s1 = s1 + fold(ex * ux + ey * uy + ez * uz)
                else:
                    uy = uy * keep_next
                    uz = uz * keep_next
                    unext_ref[pol, part, 0] = uy
                    unext_ref[pol, part, 1] = uz
                if u_old is not None:
                    px, py, pz = u_old
                    fx = st.face_x(py, pz)
                    fy, fz = st.faces_yz(px, py, pz, uy, uz)
                    face_ref[pol, part, 0, i - 1] = fx
                    face_ref[pol, part, 1, i - 1] = fy
                    face_ref[pol, part, 2, i - 1] = fz
                    qx, qy, qz = px * px, py * py, pz * pz
                    s2 = s2 + fold(qx + qy + qz)
                    total = fx * fx + fy * fy + fz * fz + st.edge_terms(qx, qy, qz)
                    if i == 1:
                        total = total + is_first * (qy + qz)
                    s3 = s3 + fold(total)
                if i < PLANES:
                    u_old = (ux, uy, uz)
        acc_ref[pol, 0] = s0
        acc_ref[pol, 1] = s1
        acc_ref[pol, 2] = s2
        acc_ref[pol, 3] = s3
        for i in range(PLANES):
            br = [b_ref[pol, 0, c, i] for c in range(3)]
            bi = [b_ref[pol, 1, c, i] for c in range(3)]
            ur = [u_ref[pol, 0, c, i] for c in range(3)]
            ui = [u_ref[pol, 1, c, i] for c in range(3)]
            t_ref[pol, 0, i] = dot3(br, br) - dot3(bi, bi)
            t_ref[pol, 1, i] = dot3(ur, ur) - dot3(ui, ui)
            t_ref[pol, 2, i] = dot3(br, ur) - dot3(bi, ui)
        return carry

    lax.fori_loop(0, 2, one_pol, 0)


N_SUMS = 12


def moment_kernel(got_ref, b_ref, high_ref, u_ref, face_ref, acc_ref, sigma_ref, sums_ref, next_ref):
    st = Stencil()
    is_first = jnp.where(lax.axis_index("space") == 0, 1.0, 0.0).astype(F32)
    group = iota(1, (DEPTH, 128)) // SLAB
    for half in range(2):
        cols = pl.ds(128 * half, 128)
        for i in range(PLANES + 1):
            value = None
            for q in range(4):
                piece = got_ref[4 * half + q, 0 if i < PLANES else 1]
                shift = (SLAB * (q - i)) % 128 if i < PLANES else 0
                piece = pltpu.roll(piece, shift, 1) if shift else piece
                value = piece if value is None else jnp.where(group == q, piece, value)
            if i < PLANES:
                sigma_ref[i, :, cols] = value
            else:
                next_ref[:, cols] = value

    lane = iota(1, (1, 128))

    def one_pol(pol, row):
        names = ("d1", "d2", "d3", "e1", "e2", "g", "x1", "x2")
        acc = {name: jnp.zeros((8, 128), F32) for name in names}

        def add(name, plane):
            acc[name] = acc[name] + fold(plane)

        for part in range(2):
            after = next_ref[...]
            wy_next = after * high_ref[pol, part, 1]
            wz_next = after * high_ref[pol, part, 2]
            for i in reversed(range(PLANES)):
                s = sigma_ref[i]
                b = [b_ref[pol, part, c, i] for c in range(3)]
                u = [u_ref[pol, part, c, i] for c in range(3)]
                w = [s * f for f in b]
                fx = st.face_x(w[1], w[2])
                fy, fz = st.faces_yz(w[0], w[1], w[2], wy_next, wz_next)
                wy_next, wz_next = w[1], w[2]
                gx, gy, gz = [face_ref[pol, part, c, i] for c in range(3)]
                rx, ry, rz = [f * f for f in w]
                qx, qy, qz = [f * v for f, v in zip(w, u)]
                ww = rx + ry + rz
                uw = qx + qy + qz
                x1 = fx * gx + fy * gy + fz * gz + st.edge_terms(qx, qy, qz)
                x2 = fx * fx + fy * fy + fz * fz + st.edge_terms(rx, ry, rz)
                if i == 0:
                    x1 = x1 + is_first * (qy + qz)
                    x2 = x2 + is_first * (ry + rz)
                add("x1", x1)
                add("x2", x2)
                add("d1", dot3(w, b))
                add("d2", ww)
                add("d3", s * ww)
                add("e1", uw)
                add("e2", s * dot3(u, u))
                add("g", s * uw)
        every = [acc_ref[pol, k] for k in range(4)] + [acc[name] for name in names]
        for k, value in enumerate(every):
            row = row + jnp.where(lane == k + 64 * pol, jnp.sum(value, axis=(0, 1), keepdims=True), 0.0)
        return row

    row = lax.fori_loop(0, 2, one_pol, jnp.zeros((1, 128), F32))
    for k in range(N_SPACE):
        sums_ref[k] = row


def times(a, b):
    return a[0] * b[0] - a[1] * b[1], a[0] * b[1] + a[1] * b[0]


def over(a, b):
    denom = b[0] * b[0] + b[1] * b[1]
    return (a[0] * b[0] + a[1] * b[1]) / denom, (a[1] * b[0] - a[0] * b[1]) / denom


def steps(sums_ref, omega):
    row = jnp.sum(jnp.concatenate([sums_ref[k] for k in range(N_SPACE)], axis=0), axis=0, keepdims=True)
    found = []
    for pol in range(2):
        s0, s1, s2, s3, d1, d2, d3, e1, e2, g, x1, x2 = [
            row[:, k + 64 * pol : k + 64 * pol + 1] for k in range(N_SUMS)
        ]
        w2 = omega * omega
        m0 = (s0, jnp.zeros_like(s0))
        m1 = (s1, omega * d1)
        m2 = (s2 - w2 * d2, 2.0 * omega * e1)
        m3 = (s3 - w2 * (2.0 * g + x2), omega * (2.0 * x1 + e2) - omega * w2 * d3)
        a0 = over(m0, m1)
        a0a0 = times(a0, a0)
        z = times(a0a0, m2)
        rho = (z[0] - s0, z[1])
        grow = (1.0 + rho[0] / s0, rho[1] / s0)
        first = times(times(grow, grow), m1)
        second = times(times(a0, grow), m2)
        third = times(a0a0, m3)
        curv = (first[0] - 2.0 * second[0] + third[0], first[1] - 2.0 * second[1] + third[1])
        a1 = over(rho, curv)
        a1g = times(a1, grow)
        a1a0 = times(a1, a0)
        found.append(((a0[0] + a1g[0], a0[1] + a1g[1]), (-a1a0[0], -a1a0[1])))
    return found


def sense_kernel(omega_ref, sums_ref, t_ref, sigma_ref, out_ref):
    omega = omega_ref[0]
    found = steps(sums_ref, omega)
    group = iota(1, (DEPTH, 128)) // SLAB
    planes = []
    for i in range(PLANES):
        scaled = omega * sigma_ref[i]
        total = jnp.zeros((DEPTH, WIDTH), F32)
        for pol in range(2):
            c0, c1 = found[pol]
            fr = c0[0] - scaled * c1[1]
            fi = c0[1] + scaled * c1[0]
            total = total + (fr * fr + fi * fi) * t_ref[pol, 0, i]
            total = total + (c1[0] * c1[0] + c1[1] * c1[1]) * t_ref[pol, 1, i]
            total = total + 2.0 * (fr * c1[0] + fi * c1[1]) * t_ref[pol, 2, i]
        planes.append(omega * total)
    for f in range(N_FREQ):
        half, q = f // 4, f % 4
        value = None
        for i in range(PLANES):
            piece = planes[i][:, 128 * half : 128 * half + 128]
            shift = (SLAB * (i - q)) % 128
            piece = pltpu.roll(piece, shift, 1) if shift else piece
            value = piece if value is None else jnp.where(group == i, piece, value)
        out_ref[f] = value


def field_kernel(omega_ref, sums_ref, b_ref, u_ref, sigma_ref, cells_ref, depth_ref, x_ref, sampled_ref):
    omega = omega_ref[0]
    found = steps(sums_ref, omega)
    cells, depth = cells_ref[...], depth_ref[...]
    stations = cells.shape[1]
    in_row = iota(0, (PLANES * DEPTH, stations)) == cells // WIDTH * DEPTH + depth
    in_lane = (iota(0, (WIDTH, stations)) == cells % WIDTH).astype(F32)
    for pol in range(2):
        c0, c1 = found[pol]
        for i in range(PLANES):
            scaled = omega * sigma_ref[i]
            fr = c0[0] - scaled * c1[1]
            fi = c0[1] + scaled * c1[0]
            for c in range(3):
                br, bi = b_ref[pol, 0, c, i], b_ref[pol, 1, c, i]
                ur, ui = u_ref[pol, 0, c, i], u_ref[pol, 1, c, i]
                x_ref[pol, 0, c, i] = fr * br - fi * bi + c1[0] * ur - c1[1] * ui
                x_ref[pol, 1, c, i] = fr * bi + fi * br + c1[0] * ui + c1[1] * ur
        for part in range(2):
            for c in range(3):
                rows = x_ref[pol, part, c].reshape(PLANES * DEPTH, WIDTH)
                picked = jnp.dot(rows, in_lane, precision=lax.Precision.HIGHEST, preferred_element_type=F32)
                sampled_ref[pol, part, pl.ds(c, 1)] = jnp.sum(
                    jnp.where(in_row, picked, 0.0), axis=0, keepdims=True
                )


def gradient_kernel(terms_ref, own_ref, out_ref):
    total = terms_ref[0]
    for f in range(1, N_FREQ):
        total = total + terms_ref[f]
    for i in range(PLANES):
        out_ref[i] = own_ref[i] * total[:, SLAB * i : SLAB * i + SLAB] * (1.0 / (3.0 * 2 * N_FREQ))


def shape(*dims):
    return jax.ShapeDtypeStruct(dims, F32)


def cost(us):
    return pl.CostEstimate(flops=0, bytes_accessed=int(us * 3.0e6), transcendentals=0)


def local(source_current, conductivity, frequency, station_cells, station_depth):
    b = source_current[0]
    stations = station_cells.shape[0]
    ends = N_SPACE - 1
    upward = [(i, i + 1) for i in range(ends)]
    downward = [(i + 1, i) for i in range(ends)]

    next_sigma = lax.ppermute(conductivity[:1], "space", downward)
    to_left, to_right = pl.pallas_call(
        send_kernel,
        out_shape=(shape(2, 2, 5, DEPTH, WIDTH), shape(2, 2, 3, DEPTH, WIDTH)),
        in_specs=[anywhere()],
        out_specs=(anywhere(), anywhere()),
        scratch_shapes=[pltpu.SemaphoreType.DMA((3,))],
        compiler_params=params(),
        name="halo_planes",
    )(b)
    high = lax.ppermute(to_left, "space", downward)
    low = lax.ppermute(to_right, "space", upward)
    packed = pl.pallas_call(
        pack_kernel,
        out_shape=shape(N_FREQ, 2, DEPTH, 128),
        in_specs=[vmem(), vmem()],
        out_specs=vmem(),
        compiler_params=params(),
        name="pack_conductivity",
    )(conductivity, next_sigma)
    got = lax.all_to_all(packed, "freq", 0, 0)

    u, _, faces, products, acc = pl.pallas_call(
        curl_kernel,
        out_shape=(
            shape(2, 2, 3, PLANES, DEPTH, WIDTH),
            shape(2, 2, 2, DEPTH, WIDTH),
            shape(2, 2, 3, PLANES, DEPTH, WIDTH),
            shape(2, 3, PLANES, DEPTH, WIDTH),
            shape(2, 4, 8, 128),
        ),
        in_specs=[vmem()] * 3,
        out_specs=(vmem(),) * 5,
        compiler_params=params(),
        cost_estimate=cost(3.0),
        name="curl_curl",
    )(b, low, high)
    sigma, sums = pl.pallas_call(
        moment_kernel,
        out_shape=(shape(PLANES, DEPTH, WIDTH), shape(N_SPACE, 1, 128)),
        in_specs=[vmem()] * 6,
        out_specs=(vmem(),) * 2,
        scratch_shapes=[pltpu.VMEM((DEPTH, WIDTH), F32)],
        compiler_params=params(),
        cost_estimate=cost(2.0),
        name="moments",
    )(got, b, high, u, faces, acc)
    all_sums = lax.all_to_all(sums, "space", 0, 0)
    terms = pl.pallas_call(
        sense_kernel,
        out_shape=shape(N_FREQ, DEPTH, 128),
        in_specs=[smem()] + [vmem()] * 3,
        out_specs=vmem(),
        compiler_params=params(),
        cost_estimate=cost(1.0),
        name="sensitivity",
    )(frequency, all_sums, products, sigma)
    shared = lax.all_to_all(terms, "freq", 0, 0)
    x, sampled = pl.pallas_call(
        field_kernel,
        out_shape=(shape(2, 2, 3, PLANES, DEPTH, WIDTH), shape(2, 2, 3, stations)),
        in_specs=[smem()] + [vmem()] * 6,
        out_specs=(vmem(),) * 2,
        compiler_params=params(),
        cost_estimate=cost(3.0),
        name="field",
    )(frequency, all_sums, b, u, sigma, station_cells[None], station_depth[None])
    gradient = pl.pallas_call(
        gradient_kernel,
        out_shape=shape(PLANES, DEPTH, SLAB),
        in_specs=[vmem()] * 2,
        out_specs=vmem(),
        compiler_params=params(),
        name="gradient",
    )(shared, conductivity)
    return x[None], sampled[None], gradient


def solution(mesh):
    return jax.shard_map(
        local,
        mesh=mesh,
        in_specs=(
            P("freq", None, None, None, "space", None, None),
            P("space", None, "freq"),
            P("freq"),
            P("space"),
            P("space"),
        ),
        out_specs=(
            P("freq", None, None, None, "space", None, None),
            P("freq", None, None, None, "space"),
            P("space", None, "freq"),
        ),
        check_vma=False,
    )
```

time: 336 us -> 62.3 us (0.19)
  blocking collectives: 197 us -> 0 us
  waiting for transfers between devices: 76.3 us -> 18 us
  starting transfers between devices: 10.9 us -> 30.3 us
  other arithmetic: 18 us -> 0 us
  between operations: 15.1 us -> 1.38 us
  local copies, waits for them, and re-layouts: 17 us -> 3.85 us
  Pallas kernels: 0 us -> 8.2 us
    psum x3 -> x0, blocking collectives: 164 us -> none  [the longest x2 111 us: local(): curvature = lax.psum(inner_product(shadow_dir, image), 'space')]
    unnamed x2 -> x0, waiting for transfers between devices: 69.8 us -> none
    all_gather x1 -> x0, blocking collectives: 33.6 us -> none  [local(): whole_sigma = lax.all_gather(conductivity, 'freq', axis=2, tiled=True)]
    all_to_all x0 -> x3, starting transfers between devices: none -> 20.7 us  [the longest x1 11.4 us: local(): all_sums = lax.all_to_all(sums, 'space', 0, 0)]
    all_to_all x0 -> x3, waiting for transfers between devices: none -> 15.5 us  [the longest x1 7.13 us: local(): all_sums = lax.all_to_all(sums, 'space', 0, 0)]
    pallas_call x0 -> x7, Pallas kernels: none -> 8.2 us  [the longest x1 1.92 us: local(): pl.pallas_call(field_kernel, out_shape=(shape(2, 2, 3, PLANES, DEPTH, WID...]
    add x3 -> x0, local copies, waits for them, and re-layouts: 4.88 us -> none  [local(): solution = solution + scale_field(step_size, direction)]
    concatenate x2 -> x0, other arithmetic: 4.87 us -> none  [with_halo(): jnp.concatenate([lax.ppermute(tail, axis, [(i, (i + 1) % count) for i in...]
  transfers between devices with their start and end apart: 5 -> 6, of which waited for: 3 -> 4; matrix products, arithmetic and copies ran while one was open for 3% -> 2% of each run, Pallas kernels for 0% -> 7%
where the time goes in v1:
time: 62.3 us; the launch traced here: 61.8 us
  starting transfers between devices  30.3 us (49%)
  waiting for transfers between devices  18 us (29%)
  Pallas kernels  8.2 us (13%)
  local copies, waits for them, and re-layouts  3.85 us (6%)
  between operations  1.38 us (2%)
    all_to_all x1, starting transfers between devices, local(): all_sums = lax.all_to_all(sums, 'space', 0, 0)  11.4 us
    all_to_all x1, waiting for transfers between devices, local(): all_sums = lax.all_to_all(sums, 'space', 0, 0)  7.13 us
    all_to_all x1, starting transfers between devices, local(): got = lax.all_to_all(packed, 'freq', 0, 0)  5.97 us
    ppermute x1, starting transfers between devices, local(): high = lax.ppermute(to_left, 'space', downward)  5.28 us
    all_to_all x1, waiting for transfers between devices, local(): got = lax.all_to_all(packed, 'freq', 0, 0)  4.98 us
    all_to_all x1, starting transfers between devices, local(): shared = lax.all_to_all(terms, 'freq', 0, 0)  3.35 us
    all_to_all x1, waiting for transfers between devices, local(): shared = lax.all_to_all(terms, 'freq', 0, 0)  3.35 us
    unnamed x13, local copies, waits for them, and re-layouts  3.15 us
  transfers between devices with their start and end apart: 6, of which 4 were waited for; matrix products, arithmetic and copies ran while one was open for 2% of the time, Pallas kernels for 7%

profile of v1, /device:TPU:1, one launch (start us, length us, event | category | flops | bytes accessed | tf_op | source)
XLA Modules:
  0.0 61.8 jit_solution(5653020066670763575)
XLA Ops:
  0.6 0.0 copy-start
  0.6 1.1 %copy-done = f32[1,2,2,3,4,16,256]{6,5,4,3,2,1,0:T(8,128)S(1)} copy-done((f32[1,2,2,3,4,16,256]{6,5,4,3,2,1,0:T(8,128)S(1)}, f32[1,2,2,3,4,16,256]{6,5,4,3,2,1,0:T(8,128)}, u32[]{:S(2)}) %copy-start) | copy-done | bytes 786456
  1.8 0.0 copy-start.1
  1.8 0.1 halo_planes.1
  1.9 5.3 %collective-permute-start.1 = (f32[2,2,5,16,256]{4,3,2,1,0:T(8,128)S(1)}, f32[2,2,5,16,256]{4,3,2,1,0:T(8,128)S(1)}, u32[]{:S(2)}, u32[]{:S(2)}) collective-permute-start(f32[2,2,5,16,256]{4,3,2,1,0:T(8,128)S(1)} %get-tuple-element.13), channel_id=1, source_target_pairs={{1,0},{2,1},{3,2},{4,3},{5,4},{6,5},{7,6},{8,7},{9,8},{10,9},{11,1... | collective-permute-start | bytes 983048 | tf_op jit(solution)/shard_map/ppermute | solution.py:364
  7.2 1.9 %collective-permute-start.2 = (f32[2,2,3,16,256]{4,3,2,1,0:T(8,128)S(1)}, f32[2,2,3,16,256]{4,3,2,1,0:T(8,128)S(1)}, u32[]{:S(2)}, u32[]{:S(2)}) collective-permute-start(f32[2,2,3,16,256]{4,3,2,1,0:T(8,128)S(1)} %get-tuple-element.14), channel_id=1, source_target_pairs={{0,1},{1,2},{2,3},{3,4},{4,5},{5,6},{6,7},{7,8},{8,9},{9,10},{10,1... | collective-permute-start | bytes 589832 | tf_op jit(solution)/shard_map/ppermute | solution.py:365
  9.1 0.7 %slice.3 = f32[1,16,32]{2,1,0:T(8,128)S(1)} slice(f32[4,16,32]{2,1,0:T(8,128)} %own_ref.3), slice={[0:1], [0:16], [0:32]} | slice | bytes 4096 | tf_op jit(solution)/shard_map/slice | solution.py:354
  9.8 2.4 %collective-permute-start = (f32[1,16,32]{2,1,0:T(8,128)S(1)}, f32[1,16,32]{2,1,0:T(8,128)S(1)}, u32[]{:S(2)}, u32[]{:S(2)}) collective-permute-start(f32[1,16,32]{2,1,0:T(8,128)S(1)} %slice.3), channel_id=1, source_target_pairs={{1,0},{2,1},{3,2},{4,3},{5,4},{6,5},{7,6},{8,7},{9,8},{10,9},{11,1... | collective-permute-start | bytes 6152 | tf_op jit(solution)/shard_map/ppermute | solution.py:354
  12.2 2.5 %collective-permute-done.next_ref = f32[1,16,32]{2,1,0:T(8,128)S(1)} collective-permute-done((f32[1,16,32]{2,1,0:T(8,128)S(1)}, f32[1,16,32]{2,1,0:T(8,128)S(1)}, u32[]{:S(2)}, u32[]{:S(2)}) %collective-permute-start) | collective-permute-done | bytes 2080 | tf_op jit(solution)/shard_map/ppermute | solution.py:354
  14.8 0.0 copy-start.2
  14.8 0.8 %copy-done.2 = f32[4,16,32]{2,1,0:T(8,128)S(1)} copy-done((f32[4,16,32]{2,1,0:T(8,128)S(1)}, f32[4,16,32]{2,1,0:T(8,128)}, u32[]{:S(2)}) %copy-start.2) | copy-done | bytes 8216
  15.5 0.7 %pack_conductivity.1 = f32[8,2,16,128]{3,2,1,0:T(8,128)} custom-call(f32[4,16,32]{2,1,0:T(8,128)S(1)} %copy-done.2, f32[1,16,32]{2,1,0:T(8,128)S(1)} %collective-permute-done.next_ref), custom_call_target="tpu_custom_call" | custom-call | tf_op jit(solution)/shard_map/pack_conductivity/pallas_call | solution.py:366
  16.3 6.0 %all-to-all-start = ((f32[8,2,16,128]{3,2,1,0:T(8,128)}), f32[8,2,16,128]{3,2,1,0:T(8,128)S(1)}, u32[]{:S(2)}, u32[]{:S(2)}) async-start(f32[8,2,16,128]{3,2,1,0:T(8,128)} %pack_conductivity.1), calls=%async_computation | async-start | bytes 262144 | tf_op jit(solution)/shard_map/all_to_all | solution.py:374
  22.2 0.0 collective-permute-done.2.low_ref
  22.2 0.0 collective-permute-done.1.high_ref
  22.2 0.0 copy-done.1
  22.3 1.8 %curl_curl.1 = (f32[2,2,3,4,16,256]{5,4,3,2,1,0:T(8,128)S(1)}, f32[2,2,2,16,256]{4,3,2,1,0:T(8,128)}, f32[2,2,3,4,16,256]{5,4,3,2,1,0:T(8,128)S(1)}, f32[2,3,4,1...) custom-call(f32[2,2,3,4,16,256]{5,4,3,2,1,0:T(8,128)S(1)} %bitcast.6, ...), custom_call_target="tpu_custom_call" | custom-call | bytes 9000000 | tf_op jit(solution)/shard_map/curl_curl/pallas_call | solution.py:376
  24.0 5.0 %all-to-all-done.got_ref = f32[8,2,16,128]{3,2,1,0:T(8,128)S(1)} async-done(((f32[8,2,16,128]{3,2,1,0:T(8,128)}), f32[8,2,16,128]{3,2,1,0:T(8,128)S(1)}, u32[]{:S(2)}, u32[]{:S(2)}) %all-to-all-start) | async-done | bytes 131104 | tf_op jit(solution)/shard_map/all_to_all | solution.py:374
  29.0 1.7 %moments.1 = (f32[4,16,256]{2,1,0:T(8,128)S(1)}, f32[32,1,128]{2,1,0:T(1,128)}) custom-call(f32[8,2,16,128]{3,2,1,0:T(8,128)S(1)} %all-to-all-done.got_ref, f32[2,2,3,4,16,256]{5,4,3,2,1,0:T(8,128)S(1)} %bitcast.7, f32[2,2,5,16,256]{4,3,2,1,0:T(8,128)S(1)} %collective-permute-done.1.high_ref, f32[2,2,3,4,16,256]{5,4,3,2,1,0:T(8,128)S(1)} %get-tuple-element.15.u_ref, ...), custom_call_target="tpu_custom_call" | custom-call | bytes 6000000 | tf_op jit(solution)/shard_map/moments/pallas_call | solution.py:391
  30.6 11.4 %all-to-all-start.1 = ((f32[32,1,128]{2,1,0:T(1,128)}), f32[32,1,128]{2,1,0:T(1,128)S(1)}, u32[]{:S(2)}, u32[]{:S(2)}) async-start(f32[32,1,128]{2,1,0:T(1,128)} %get-tuple-element.18), calls=%async_computation.1 | async-start | bytes 32768 | tf_op jit(solution)/shard_map/all_to_all | solution.py:401
  42.7 7.1 %all-to-all-done.1.sums_ref = f32[32,1,128]{2,1,0:T(1,128)S(1)} async-done(((f32[32,1,128]{2,1,0:T(1,128)}), f32[32,1,128]{2,1,0:T(1,128)S(1)}, u32[]{:S(2)}, u32[]{:S(2)}) %all-to-all-start.1) | async-done | bytes 16416 | tf_op jit(solution)/shard_map/all_to_all | solution.py:401
  49.8 1.3 %sensitivity.1 = f32[8,16,128]{2,1,0:T(8,128)} custom-call(f32[1]{0:T(128)S(6)} %copy.9.omega_ref, f32[32,1,128]{2,1,0:T(1,128)S(1)} %all-to-all-done.1.sums_ref, f32[2,3,4,16,256]{4,3,2,1,0:T(8,128)S(1)} %get-tuple-element.22.t_ref, f32[4,16,256]{2,1,0:T(8,128)S(1)} %get-tuple-element.19.sigma_ref), custom_call_target="tpu_custom_call" | custom-call | bytes 3000000 | tf_op jit(solution)/shard_map/sensitivity/pallas_call | solution.py:402
  51.2 3.3 %all-to-all-start.2 = ((f32[8,16,128]{2,1,0:T(8,128)}), f32[8,16,128]{2,1,0:T(8,128)S(1)}, u32[]{:S(2)}, u32[]{:S(2)}) async-start(f32[8,16,128]{2,1,0:T(8,128)} %sensitivity.1), calls=%async_computation.2 | async-start | bytes 131072 | tf_op jit(solution)/shard_map/all_to_all | solution.py:411
  54.5 0.0 copy-start.4
  54.5 0.0 copy-start.5
  54.5 0.6 %copy-done.4 = s32[64]{0:T(128)S(1)} copy-done((s32[64]{0:T(128)S(1)}, s32[64]{0:T(128)}, u32[]{:S(2)}) %copy-start.4) | copy-done | bytes 280
  55.2 0.0 copy-done.5
  55.2 0.0 copy-start.3
  55.2 1.9 %field.1 = (f32[2,2,3,4,16,256]{5,4,3,2,1,0:T(8,128)}, f32[2,2,3,64]{3,2,1,0:T(4,128)S(1)}) custom-call(f32[1]{0:T(128)S(6)} %copy.9.omega_ref, f32[32,1,128]{2,1,0:T(1,128)S(1)} %all-to-all-done.1.sums_ref, f32[2,2,3,4,16,256]{5,4,3,2,1,0:T(8,128)S(1)} %bitcast.8, f32[2,2,3,4,16,256]{5,4,3,2,1,0:T(8,128)S(1)} %get-tuple-element.15.u_ref, ...), custom_call_target="tpu_custom_call" | custom-call | bytes 9000000 | tf_op jit(solution)/shard_map/field/pallas_call | solution.py:412
  57.1 0.6 copy.8
  57.7 3.3 %all-to-all-done.2.terms_ref = f32[8,16,128]{2,1,0:T(8,128)S(1)} async-done(((f32[8,16,128]{2,1,0:T(8,128)}), f32[8,16,128]{2,1,0:T(8,128)S(1)}, u32[]{:S(2)}, u32[]{:S(2)}) %all-to-all-start.2) | async-done | bytes 65568 | tf_op jit(solution)/shard_map/all_to_all | solution.py:411
  61.1 0.0 copy-done.3
  61.1 0.7 %gradient.1 = f32[4,16,32]{2,1,0:T(8,128)} custom-call(f32[8,16,128]{2,1,0:T(8,128)S(1)} %all-to-all-done.2.terms_ref, f32[4,16,32]{2,1,0:T(8,128)S(1)} %copy-done.3), custom_call_target="tpu_custom_call" | custom-call | tf_op jit(solution)/shard_map/gradient/pallas_call | solution.py:421
Async XLA Ops:
  0.6 1.1 %copy-start = (f32[1,2,2,3,4,16,256]{6,5,4,3,2,1,0:T(8,128)S(1)}, f32[1,2,2,3,4,16,256]{6,5,4,3,2,1,0:T(8,128)}, u32[]{:S(2)}) copy-start(f32[1,2,2,3,4,16,256]{6,5,4,3,2,1,0:T(8,128)} %param.5) | copy-start | bytes 2359300
  1.8 20.5 %copy-start.1 = (f32[1,2,2,3,4,16,256]{6,5,4,3,2,1,0:T(8,128)S(1)}, f32[1,2,2,3,4,16,256]{6,5,4,3,2,1,0:T(8,128)}, u32[]{:S(2)}) copy-start(f32[1,2,2,3,4,16,256]{6,5,4,3,2,1,0:T(8,128)} %param.5) | copy-start | bytes 2359300
  1.9 20.4 %collective-permute-start.1 = (f32[2,2,5,16,256]{4,3,2,1,0:T(8,128)S(1)}, f32[2,2,5,16,256]{4,3,2,1,0:T(8,128)S(1)}, u32[]{:S(2)}, u32[]{:S(2)}) collective-permute-start(f32[2,2,5,16,256]{4,3,2,1,0:T(8,128)S(1)} %get-tuple-element.13), channel_id=1, source_target_pairs={{1,0},{2,1},{3,2},{4,3},{5,4},{6,5},{7,6},{8,7},{9,8},{10,9},{11,1... | collective-permute-start | bytes 983048 | tf_op jit(solution)/shard_map/ppermute | solution.py:364
  7.2 15.1 %collective-permute-start.2 = (f32[2,2,3,16,256]{4,3,2,1,0:T(8,128)S(1)}, f32[2,2,3,16,256]{4,3,2,1,0:T(8,128)S(1)}, u32[]{:S(2)}, u32[]{:S(2)}) collective-permute-start(f32[2,2,3,16,256]{4,3,2,1,0:T(8,128)S(1)} %get-tuple-element.14), channel_id=1, source_target_pairs={{0,1},{1,2},{2,3},{3,4},{4,5},{5,6},{6,7},{7,8},{8,9},{9,10},{10,1... | collective-permute-start | bytes 589832 | tf_op jit(solution)/shard_map/ppermute | solution.py:365
  9.8 5.0 %collective-permute-start = (f32[1,16,32]{2,1,0:T(8,128)S(1)}, f32[1,16,32]{2,1,0:T(8,128)S(1)}, u32[]{:S(2)}, u32[]{:S(2)}) collective-permute-start(f32[1,16,32]{2,1,0:T(8,128)S(1)} %slice.3), channel_id=1, source_target_pairs={{1,0},{2,1},{3,2},{4,3},{5,4},{6,5},{7,6},{8,7},{9,8},{10,9},{11,1... | collective-permute-start | bytes 6152 | tf_op jit(solution)/shard_map/ppermute | solution.py:354
  14.8 0.8 %copy-start.2 = (f32[4,16,32]{2,1,0:T(8,128)S(1)}, f32[4,16,32]{2,1,0:T(8,128)}, u32[]{:S(2)}) copy-start(f32[4,16,32]{2,1,0:T(8,128)} %own_ref.3) | copy-start | bytes 24580
  16.3 12.7 %all-to-all-start = ((f32[8,2,16,128]{3,2,1,0:T(8,128)}), f32[8,2,16,128]{3,2,1,0:T(8,128)S(1)}, u32[]{:S(2)}, u32[]{:S(2)}) async-start(f32[8,2,16,128]{3,2,1,0:T(8,128)} %pack_conductivity.1), calls=%async_computation | async-start | bytes 262144 | tf_op jit(solution)/shard_map/all_to_all | solution.py:374
  30.6 19.2 %all-to-all-start.1 = ((f32[32,1,128]{2,1,0:T(1,128)}), f32[32,1,128]{2,1,0:T(1,128)S(1)}, u32[]{:S(2)}, u32[]{:S(2)}) async-start(f32[32,1,128]{2,1,0:T(1,128)} %get-tuple-element.18), calls=%async_computation.1 | async-start | bytes 32768 | tf_op jit(solution)/shard_map/all_to_all | solution.py:401
  51.2 9.9 %all-to-all-start.2 = ((f32[8,16,128]{2,1,0:T(8,128)}), f32[8,16,128]{2,1,0:T(8,128)S(1)}, u32[]{:S(2)}, u32[]{:S(2)}) async-start(f32[8,16,128]{2,1,0:T(8,128)} %sensitivity.1), calls=%async_computation.2 | async-start | bytes 131072 | tf_op jit(solution)/shard_map/all_to_all | solution.py:411
  54.5 0.7 %copy-start.4 = (s32[64]{0:T(128)S(1)}, s32[64]{0:T(128)}, u32[]{:S(2)}) copy-start(s32[64]{0:T(128)} %param.8) | copy-start | bytes 772
  54.5 0.7 %copy-start.5 = (s32[64]{0:T(128)S(1)}, s32[64]{0:T(128)}, u32[]{:S(2)}) copy-start(s32[64]{0:T(128)} %param.9) | copy-start | bytes 772
  55.2 5.9 %copy-start.3 = (f32[4,16,32]{2,1,0:T(8,128)S(1)}, f32[4,16,32]{2,1,0:T(8,128)}, u32[]{:S(2)}) copy-start(f32[4,16,32]{2,1,0:T(8,128)} %own_ref.3) | copy-start | bytes 24580

commit v2 on v1

--- a/solution.py
+++ b/solution.py
@@ -73,27 +73,37 @@
     return a[0] * b[0] + a[1] * b[1] + a[2] * b[2]
 
 
-def send_kernel(b_ref, right_ref, left_ref, sems):
-    copies = [
-        pltpu.make_async_copy(b_ref.at[:, :, :, 0], right_ref.at[:, :, pl.ds(0, 3)], sems.at[0]),
-        pltpu.make_async_copy(b_ref.at[:, :, pl.ds(1, 2), 1], right_ref.at[:, :, pl.ds(3, 2)], sems.at[1]),
-        pltpu.make_async_copy(b_ref.at[:, :, :, PLANES - 1], left_ref, sems.at[2]),
-    ]
-    for copy in copies:
-        copy.start()
-    for copy in copies:
-        copy.wait()
-
-
-def pack_kernel(own_ref, next_ref, out_ref):
+LAST = PLANES - 1
+SLAB_PLANE = 16
+
+
+def send_kernel(b_ref, own_ref, left_ref, right_ref):
+    st = Stencil()
+    for pol in range(2):
+        for part in range(2):
+            k = 2 * pol + part
+            ex, ey, ez = [b_ref[pol, part, c, 0] for c in range(3)]
+            hx = st.face_x(ey, ez)
+            hy, hz = st.faces_yz(ex, ey, ez, b_ref[pol, part, 1, 1], b_ref[pol, part, 2, 1])
+            left_ref[4 * k] = ey
+            left_ref[4 * k + 1] = ez
+            left_ref[4 * k + 2] = st.bz(hx, -ey) - hz
+            left_ref[4 * k + 3] = hy - st.by(hx, ez)
+            ex, ey, ez = [b_ref[pol, part, c, LAST] for c in range(3)]
+            right_ref[2 * k] = st.fz(ex) + ez
+            right_ref[2 * k + 1] = -ey - st.fy(ex)
+    front = jnp.concatenate([own_ref[0]] * 4, axis=1)
+    left_ref[SLAB_PLANE] = jnp.concatenate([front, front], axis=1)
+
+
+def pack_kernel(own_ref, high_ref, out_ref):
     own = jnp.concatenate([own_ref[i] for i in range(PLANES)], axis=1)
-    after = jnp.concatenate([next_ref[0]] * PLANES, axis=1)
     for f in range(N_FREQ):
         out_ref[f, 0] = own
-        out_ref[f, 1] = after
-
-
-def curl_kernel(b_ref, low_ref, high_ref, u_ref, unext_ref, face_ref, t_ref, acc_ref):
+        out_ref[f, 1] = high_ref[SLAB_PLANE, :, :128]
+
+
+def curl_kernel(b_ref, low_ref, high_ref, u_ref, face_ref, t_ref, acc_ref):
     st = Stencil()
     place = lax.axis_index("space")
     keep_next = jnp.where(place == N_SPACE - 1, 0.0, 1.0).astype(F32)
@@ -105,25 +115,22 @@
         s2 = jnp.zeros((8, 128), F32)
         s3 = jnp.zeros((8, 128), F32)
         for part in range(2):
+            k = 2 * pol + part
+
             def field(c, i):
-                if i < 0:
-                    return low_ref[pol, part, c]
-                if i < PLANES:
-                    return b_ref[pol, part, c, i]
-                if i == PLANES:
-                    return high_ref[pol, part, c]
-                return high_ref[pol, part, c + 2]
-
-            hy_old, hz_old = st.faces_yz(field(0, -1), field(1, -1), field(2, -1), field(1, 0), field(2, 0))
+                return b_ref[pol, part, c, i] if i < PLANES else high_ref[4 * k + c - 1]
+
+            hy_old = low_ref[2 * k] - field(2, 0)
+            hz_old = low_ref[2 * k + 1] + field(1, 0)
             u_old = None
             for i in range(PLANES + 1):
-                ex, ey, ez = field(0, i), field(1, i), field(2, i)
-                hx = st.face_x(ey, ez)
-                hy, hz = st.faces_yz(ex, ey, ez, field(1, i + 1), field(2, i + 1))
-                uy = st.bz(hx, -ey) - (hz - hz_old)
-                uz = (hy - hy_old) - st.by(hx, ez)
-                hy_old, hz_old = hy, hz
                 if i < PLANES:
+                    ex, ey, ez = field(0, i), field(1, i), field(2, i)
+                    hx = st.face_x(ey, ez)
+                    hy, hz = st.faces_yz(ex, ey, ez, field(1, i + 1), field(2, i + 1))
+                    uy = st.bz(hx, -ey) - (hz - hz_old)
+                    uz = (hy - hy_old) - st.by(hx, ez)
+                    hy_old, hz_old = hy, hz
                     ux = st.by(hz, -ex) - st.bz(hy, ex)
                     u_ref[pol, part, 0, i] = ux
                     u_ref[pol, part, 1, i] = uy
@@ -131,10 +138,8 @@
                     s0 = s0 + fold(ex * ex + ey * ey + ez * ez)
                     s1 = s1 + fold(ex * ux + ey * uy + ez * uz)
                 else:
-                    uy = uy * keep_next
-                    uz = uz * keep_next
-                    unext_ref[pol, part, 0] = uy
-                    unext_ref[pol, part, 1] = uz
+                    uy = keep_next * (high_ref[4 * k + 2] + hz_old)
+                    uz = keep_next * (high_ref[4 * k + 3] - hy_old)
                 if u_old is not None:
                     px, py, pz = u_old
                     fx = st.face_x(py, pz)
@@ -199,8 +204,8 @@
 
         for part in range(2):
             after = next_ref[...]
-            wy_next = after * high_ref[pol, part, 1]
-            wz_next = after * high_ref[pol, part, 2]
+            wy_next = after * high_ref[4 * (2 * pol + part)]
+            wz_next = after * high_ref[4 * (2 * pol + part) + 1]
             for i in reversed(range(PLANES)):
                 s = sigma_ref[i]
                 b = [b_ref[pol, part, c, i] for c in range(3)]
@@ -341,7 +346,7 @@
 
 
 def cost(us):
-    return pl.CostEstimate(flops=0, bytes_accessed=int(us * 3.0e6), transcendentals=0)
+    return pl.CostEstimate(flops=int(us * 1.0e9), bytes_accessed=int(us * 3.0e6), transcendentals=0)
 
 
 def local(source_current, conductivity, frequency, station_cells, station_depth):
@@ -351,16 +356,14 @@
     upward = [(i, i + 1) for i in range(ends)]
     downward = [(i + 1, i) for i in range(ends)]
 
-    next_sigma = lax.ppermute(conductivity[:1], "space", downward)
     to_left, to_right = pl.pallas_call(
         send_kernel,
-        out_shape=(shape(2, 2, 5, DEPTH, WIDTH), shape(2, 2, 3, DEPTH, WIDTH)),
-        in_specs=[anywhere()],
-        out_specs=(anywhere(), anywhere()),
-        scratch_shapes=[pltpu.SemaphoreType.DMA((3,))],
-        compiler_params=params(),
-        name="halo_planes",
-    )(b)
+        out_shape=(shape(SLAB_PLANE + 1, DEPTH, WIDTH), shape(8, DEPTH, WIDTH)),
+        in_specs=[vmem(), vmem()],
+        out_specs=(vmem(), vmem()),
+        compiler_params=params(),
+        name="edge_planes",
+    )(b, conductivity)
     high = lax.ppermute(to_left, "space", downward)
     low = lax.ppermute(to_right, "space", upward)
     packed = pl.pallas_call(
@@ -370,20 +373,19 @@
         out_specs=vmem(),
         compiler_params=params(),
         name="pack_conductivity",
-    )(conductivity, next_sigma)
+    )(conductivity, high)
     got = lax.all_to_all(packed, "freq", 0, 0)
 
-    u, _, faces, products, acc = pl.pallas_call(
+    u, faces, products, acc = pl.pallas_call(
         curl_kernel,
         out_shape=(
             shape(2, 2, 3, PLANES, DEPTH, WIDTH),
-            shape(2, 2, 2, DEPTH, WIDTH),
             shape(2, 2, 3, PLANES, DEPTH, WIDTH),
             shape(2, 3, PLANES, DEPTH, WIDTH),
             shape(2, 4, 8, 128),
         ),
         in_specs=[vmem()] * 3,
-        out_specs=(vmem(),) * 5,
+        out_specs=(vmem(),) * 4,
         compiler_params=params(),
         cost_estimate=cost(3.0),
         name="curl_curl",

time: 62.3 us -> 57.4 us (0.921)
  starting transfers between devices: 30.3 us -> 26.9 us
  local copies, waits for them, and re-layouts: 3.85 us -> 3.15 us
  Pallas kernels: 8.2 us -> 7.5 us
    ppermute x1 -> x0, waiting for transfers between devices: 2.55 us -> none  [local(): next_sigma = lax.ppermute(conductivity[:1], 'space', downward)]
    ppermute x1 -> x0, starting transfers between devices: 2.4 us -> none  [local(): next_sigma = lax.ppermute(conductivity[:1], 'space', downward)]
    ppermute x1, waiting for transfers between devices: 0.01 us -> 1.73 us  [local(): high = lax.ppermute(to_left, 'space', downward)]
    all_to_all x1, starting transfers between devices: 11.4 us -> 9.85 us  [local(): all_sums = lax.all_to_all(sums, 'space', 0, 0)]
    all_to_all x1, waiting for transfers between devices: 4.98 us -> 5.73 us  [local(): got = lax.all_to_all(packed, 'freq', 0, 0)]
    pallas_call x1, Pallas kernels: 1.75 us -> 1.01 us  [local(): pl.pallas_call(curl_kernel, out_shape=(shape(2, 2, 3, PLANES, DEPTH, WIDT...]
    slice x1 -> x0, local copies, waits for them, and re-layouts: 0.7 us -> none  [local(): next_sigma = lax.ppermute(conductivity[:1], 'space', downward)]
  transfers between devices with their start and end apart: 6 -> 5, of which waited for: 4 -> 4; matrix products, arithmetic and copies ran while one was open for 2% -> 1% of each run, Pallas kernels for 7% -> 6%
where the time goes in v2:
time: 57.4 us; the launch traced here: 57 us
  starting transfers between devices  26.9 us (47%)
  waiting for transfers between devices  18 us (31%)
  Pallas kernels  7.5 us (13%)
  local copies, waits for them, and re-layouts  3.15 us (5%)
  between operations  1.37 us (2%)
    all_to_all x1, starting transfers between devices, local(): all_sums = lax.all_to_all(sums, 'space', 0, 0)  9.85 us
    all_to_all x1, waiting for transfers between devices, local(): all_sums = lax.all_to_all(sums, 'space', 0, 0)  7.13 us
    all_to_all x1, starting transfers between devices, local(): got = lax.all_to_all(packed, 'freq', 0, 0)  6.53 us
    all_to_all x1, waiting for transfers between devices, local(): got = lax.all_to_all(packed, 'freq', 0, 0)  5.73 us
    ppermute x1, starting transfers between devices, local(): high = lax.ppermute(to_left, 'space', downward)  5.28 us
    all_to_all x1, waiting for transfers between devices, local(): shared = lax.all_to_all(terms, 'freq', 0, 0)  3.41 us
    all_to_all x1, starting transfers between devices, local(): shared = lax.all_to_all(terms, 'freq', 0, 0)  3.35 us
    unnamed x13, local copies, waits for them, and re-layouts  3.15 us
  transfers between devices with their start and end apart: 5, of which 4 were waited for; matrix products, arithmetic and copies ran while one was open for 1% of the time, Pallas kernels for 6%

profile of v2, /device:TPU:1, one launch (start us, length us, event | category | flops | bytes accessed | tf_op | source)
XLA Modules:
  0.0 57.0 jit_solution(419217126153572534)
XLA Ops:
  0.6 0.0 copy-start
  0.6 1.1 %copy-done = f32[1,2,2,3,4,16,256]{6,5,4,3,2,1,0:T(8,128)S(1)} copy-done((f32[1,2,2,3,4,16,256]{6,5,4,3,2,1,0:T(8,128)S(1)}, f32[1,2,2,3,4,16,256]{6,5,4,3,2,1,0:T(8,128)}, u32[]{:S(2)}) %copy-start) | copy-done | bytes 786456
  1.8 0.0 copy-start.2
  1.8 0.8 %copy-done.2 = f32[4,16,32]{2,1,0:T(8,128)S(1)} copy-done((f32[4,16,32]{2,1,0:T(8,128)S(1)}, f32[4,16,32]{2,1,0:T(8,128)}, u32[]{:S(2)}) %copy-start.2) | copy-done | bytes 8216
  2.5 0.0 copy-start.1
  2.5 0.2 edge_planes.1
  2.7 5.3 %collective-permute-start = (f32[17,16,256]{2,1,0:T(8,128)S(1)}, f32[17,16,256]{2,1,0:T(8,128)S(1)}, u32[]{:S(2)}, u32[]{:S(2)}) collective-permute-start(f32[17,16,256]{2,1,0:T(8,128)S(1)} %get-tuple-element.13), channel_id=1, source_target_pairs={{1,0},{2,1},{3,2},{4,3},{5,4},{6,5},{7,6},{8,7},{9,8},{10,9},{11,1... | collective-permute-start | bytes 835592 | tf_op jit(solution)/shard_map/ppermute | solution.py:367
  8.0 1.9 %collective-permute-start.1 = (f32[8,16,256]{2,1,0:T(8,128)S(1)}, f32[8,16,256]{2,1,0:T(8,128)S(1)}, u32[]{:S(2)}, u32[]{:S(2)}) collective-permute-start(f32[8,16,256]{2,1,0:T(8,128)S(1)} %get-tuple-element.14), channel_id=1, source_target_pairs={{0,1},{1,2},{2,3},{3,4},{4,5},{5,6},{6,7},{7,8},{8,9},{9,10},{10,1... | collective-permute-start | bytes 393224 | tf_op jit(solution)/shard_map/ppermute | solution.py:368
  9.9 1.7 %collective-permute-done.high_ref = f32[17,16,256]{2,1,0:T(8,128)S(1)} collective-permute-done((f32[17,16,256]{2,1,0:T(8,128)S(1)}, f32[17,16,256]{2,1,0:T(8,128)S(1)}, u32[]{:S(2)}, u32[]{:S(2)}) %collective-permute-start) | collective-permute-done | bytes 278560 | tf_op jit(solution)/shard_map/ppermute | solution.py:367
  11.6 0.7 %pack_conductivity.1 = f32[8,2,16,128]{3,2,1,0:T(8,128)} custom-call(f32[4,16,32]{2,1,0:T(8,128)S(1)} %copy-done.2, f32[17,16,256]{2,1,0:T(8,128)S(1)} %collective-permute-done.high_ref), custom_call_target="tpu_custom_call" | custom-call | tf_op jit(solution)/shard_map/pack_conductivity/pallas_call | solution.py:369
  12.4 6.5 %all-to-all-start = ((f32[8,2,16,128]{3,2,1,0:T(8,128)}), f32[8,2,16,128]{3,2,1,0:T(8,128)S(1)}, u32[]{:S(2)}, u32[]{:S(2)}) async-start(f32[8,2,16,128]{3,2,1,0:T(8,128)} %pack_conductivity.1), calls=%async_computation | async-start | bytes 262144 | tf_op jit(solution)/shard_map/all_to_all | solution.py:377
  18.9 0.0 collective-permute-done.1.low_ref
  18.9 0.0 copy-done.1
  18.9 1.0 %curl_curl.1 = (f32[2,2,3,4,16,256]{5,4,3,2,1,0:T(8,128)S(1)}, f32[2,2,3,4,16,256]{5,4,3,2,1,0:T(8,128)S(1)}, f32[2,3,4,16,256]{4,3,2,1,0:T(8,128)S(1)}, f32[2,4,8,128]{3,2,1,0:T(8,128)S(1)}) custom-call(f32[2,2,3,4,16,256]{5,4,3,2,1,0:T(8,128)S(1)} %bitcast.6, f32[8,16,256]{2,1,0:T(8,128)S(1)} %collective-permute-done.1.low_ref, ...), custom_call_target="tpu_custom_call" | custom-call | flops 3000000000 | bytes 9000000 | tf_op jit(solution)/shard_map/curl_curl/pallas_call | solution.py:379
  19.9 5.7 %all-to-all-done.got_ref = f32[8,2,16,128]{3,2,1,0:T(8,128)S(1)} async-done(((f32[8,2,16,128]{3,2,1,0:T(8,128)}), f32[8,2,16,128]{3,2,1,0:T(8,128)S(1)}, u32[]{:S(2)}, u32[]{:S(2)}) %all-to-all-start) | async-done | bytes 131104 | tf_op jit(solution)/shard_map/all_to_all | solution.py:377
  25.7 1.7 %moments.1 = (f32[4,16,256]{2,1,0:T(8,128)S(1)}, f32[32,1,128]{2,1,0:T(1,128)}) custom-call(f32[8,2,16,128]{3,2,1,0:T(8,128)S(1)} %all-to-all-done.got_ref, f32[2,2,3,4,16,256]{5,4,3,2,1,0:T(8,128)S(1)} %bitcast.7, f32[17,16,256]{2,1,0:T(8,128)S(1)} %collective-permute-done.high_ref, f32[2,2,3,4,16,256]{5,4,3,2,1,0:T(8,128)S(1)} %get-tuple-element.15.u_ref, ...), custom_call_target="tpu_custom_call" | custom-call | flops 2000000000 | bytes 6000000 | tf_op jit(solution)/shard_map/moments/pallas_call | solution.py:393
  27.3 9.8 %all-to-all-start.1 = ((f32[32,1,128]{2,1,0:T(1,128)}), f32[32,1,128]{2,1,0:T(1,128)S(1)}, u32[]{:S(2)}, u32[]{:S(2)}) async-start(f32[32,1,128]{2,1,0:T(1,128)} %get-tuple-element.18), calls=%async_computation.1 | async-start | bytes 32768 | tf_op jit(solution)/shard_map/all_to_all | solution.py:403
  37.8 7.1 %all-to-all-done.1.sums_ref = f32[32,1,128]{2,1,0:T(1,128)S(1)} async-done(((f32[32,1,128]{2,1,0:T(1,128)}), f32[32,1,128]{2,1,0:T(1,128)S(1)}, u32[]{:S(2)}, u32[]{:S(2)}) %all-to-all-start.1) | async-done | bytes 16416 | tf_op jit(solution)/shard_map/all_to_all | solution.py:403
  45.0 1.3 %sensitivity.1 = f32[8,16,128]{2,1,0:T(8,128)} custom-call(f32[1]{0:T(128)S(6)} %copy.9.omega_ref, f32[32,1,128]{2,1,0:T(1,128)S(1)} %all-to-all-done.1.sums_ref, f32[2,3,4,16,256]{4,3,2,1,0:T(8,128)S(1)} %get-tuple-element.22.t_ref, f32[4,16,256]{2,1,0:T(8,128)S(1)} %get-tuple-element.19.sigma_ref), custom_call_target="tpu_custom_call" | custom-call | flops 1000000000 | bytes 3000000 | tf_op jit(solution)/shard_map/sensitivity/pallas_call | solution.py:404
  46.3 3.3 %all-to-all-start.2 = ((f32[8,16,128]{2,1,0:T(8,128)}), f32[8,16,128]{2,1,0:T(8,128)S(1)}, u32[]{:S(2)}, u32[]{:S(2)}) async-start(f32[8,16,128]{2,1,0:T(8,128)} %sensitivity.1), calls=%async_computation.2 | async-start | bytes 131072 | tf_op jit(solution)/shard_map/all_to_all | solution.py:413
  49.6 0.0 copy-start.4
  49.7 0.0 copy-start.5
  49.7 0.6 %copy-done.4 = s32[64]{0:T(128)S(1)} copy-done((s32[64]{0:T(128)S(1)}, s32[64]{0:T(128)}, u32[]{:S(2)}) %copy-start.4) | copy-done | bytes 280
  50.3 0.0 copy-done.5
  50.3 0.0 copy-start.3
  50.3 1.9 %field.1 = (f32[2,2,3,4,16,256]{5,4,3,2,1,0:T(8,128)}, f32[2,2,3,64]{3,2,1,0:T(4,128)S(1)}) custom-call(f32[1]{0:T(128)S(6)} %copy.9.omega_ref, f32[32,1,128]{2,1,0:T(1,128)S(1)} %all-to-all-done.1.sums_ref, f32[2,2,3,4,16,256]{5,4,3,2,1,0:T(8,128)S(1)} %bitcast.8, f32[2,2,3,4,16,256]{5,4,3,2,1,0:T(8,128)S(1)} %get-tuple-element.15.u_ref, ...), custom_call_target="tpu_custom_call" | custom-call | flops 3000000000 | bytes 9000000 | tf_op jit(solution)/shard_map/field/pallas_call | solution.py:414
  52.2 0.6 %copy.8 = f32[1,2,2,3,64]{4,2,3,1,0:T(2,128)} copy(f32[1,2,2,3,64]{4,3,2,1,0:T(4,128)S(1)} %bitcast.9) | data formatting | bytes 6144
  52.8 3.4 %all-to-all-done.2.terms_ref = f32[8,16,128]{2,1,0:T(8,128)S(1)} async-done(((f32[8,16,128]{2,1,0:T(8,128)}), f32[8,16,128]{2,1,0:T(8,128)S(1)}, u32[]{:S(2)}, u32[]{:S(2)}) %all-to-all-start.2) | async-done | bytes 65568 | tf_op jit(solution)/shard_map/all_to_all | solution.py:413
  56.3 0.0 copy-done.3
  56.3 0.7 %gradient.1 = f32[4,16,32]{2,1,0:T(8,128)} custom-call(f32[8,16,128]{2,1,0:T(8,128)S(1)} %all-to-all-done.2.terms_ref, f32[4,16,32]{2,1,0:T(8,128)S(1)} %copy-done.3), custom_call_target="tpu_custom_call" | custom-call | tf_op jit(solution)/shard_map/gradient/pallas_call | solution.py:423
Async XLA Ops:
  0.6 1.1 %copy-start = (f32[1,2,2,3,4,16,256]{6,5,4,3,2,1,0:T(8,128)S(1)}, f32[1,2,2,3,4,16,256]{6,5,4,3,2,1,0:T(8,128)}, u32[]{:S(2)}) copy-start(f32[1,2,2,3,4,16,256]{6,5,4,3,2,1,0:T(8,128)} %param.5) | copy-start | bytes 2359300
  1.8 0.8 %copy-start.2 = (f32[4,16,32]{2,1,0:T(8,128)S(1)}, f32[4,16,32]{2,1,0:T(8,128)}, u32[]{:S(2)}) copy-start(f32[4,16,32]{2,1,0:T(8,128)} %own_ref.5) | copy-start | bytes 24580
  2.5 16.4 %copy-start.1 = (f32[1,2,2,3,4,16,256]{6,5,4,3,2,1,0:T(8,128)S(1)}, f32[1,2,2,3,4,16,256]{6,5,4,3,2,1,0:T(8,128)}, u32[]{:S(2)}) copy-start(f32[1,2,2,3,4,16,256]{6,5,4,3,2,1,0:T(8,128)} %param.5) | copy-start | bytes 2359300
  2.7 9.0 %collective-permute-start = (f32[17,16,256]{2,1,0:T(8,128)S(1)}, f32[17,16,256]{2,1,0:T(8,128)S(1)}, u32[]{:S(2)}, u32[]{:S(2)}) collective-permute-start(f32[17,16,256]{2,1,0:T(8,128)S(1)} %get-tuple-element.13), channel_id=1, source_target_pairs={{1,0},{2,1},{3,2},{4,3},{5,4},{6,5},{7,6},{8,7},{9,8},{10,9},{11,1... | collective-permute-start | bytes 835592 | tf_op jit(solution)/shard_map/ppermute | solution.py:367
  8.0 10.9 %collective-permute-start.1 = (f32[8,16,256]{2,1,0:T(8,128)S(1)}, f32[8,16,256]{2,1,0:T(8,128)S(1)}, u32[]{:S(2)}, u32[]{:S(2)}) collective-permute-start(f32[8,16,256]{2,1,0:T(8,128)S(1)} %get-tuple-element.14), channel_id=1, source_target_pairs={{0,1},{1,2},{2,3},{3,4},{4,5},{5,6},{6,7},{7,8},{8,9},{9,10},{10,1... | collective-permute-start | bytes 393224 | tf_op jit(solution)/shard_map/ppermute | solution.py:368
  12.4 13.3 %all-to-all-start = ((f32[8,2,16,128]{3,2,1,0:T(8,128)}), f32[8,2,16,128]{3,2,1,0:T(8,128)S(1)}, u32[]{:S(2)}, u32[]{:S(2)}) async-start(f32[8,2,16,128]{3,2,1,0:T(8,128)} %pack_conductivity.1), calls=%async_computation | async-start | bytes 262144 | tf_op jit(solution)/shard_map/all_to_all | solution.py:377
  27.3 17.6 %all-to-all-start.1 = ((f32[32,1,128]{2,1,0:T(1,128)}), f32[32,1,128]{2,1,0:T(1,128)S(1)}, u32[]{:S(2)}, u32[]{:S(2)}) async-start(f32[32,1,128]{2,1,0:T(1,128)} %get-tuple-element.18), calls=%async_computation.1 | async-start | bytes 32768 | tf_op jit(solution)/shard_map/all_to_all | solution.py:403
  46.3 10.0 %all-to-all-start.2 = ((f32[8,16,128]{2,1,0:T(8,128)}), f32[8,16,128]{2,1,0:T(8,128)S(1)}, u32[]{:S(2)}, u32[]{:S(2)}) async-start(f32[8,16,128]{2,1,0:T(8,128)} %sensitivity.1), calls=%async_computation.2 | async-start | bytes 131072 | tf_op jit(solution)/shard_map/all_to_all | solution.py:413
  49.6 0.7 %copy-start.4 = (s32[64]{0:T(128)S(1)}, s32[64]{0:T(128)}, u32[]{:S(2)}) copy-start(s32[64]{0:T(128)} %param.8) | copy-start | bytes 772
  49.7 0.7 %copy-start.5 = (s32[64]{0:T(128)S(1)}, s32[64]{0:T(128)}, u32[]{:S(2)}) copy-start(s32[64]{0:T(128)} %param.9) | copy-start | bytes 772
  50.3 5.9 %copy-start.3 = (f32[4,16,32]{2,1,0:T(8,128)S(1)}, f32[4,16,32]{2,1,0:T(8,128)}, u32[]{:S(2)}) copy-start(f32[4,16,32]{2,1,0:T(8,128)} %own_ref.5) | copy-start | bytes 24580

commit v3 on v2

--- a/solution.py
+++ b/solution.py
@@ -75,6 +75,17 @@
 
 LAST = PLANES - 1
 SLAB_PLANE = 16
+
+
+def placed(parts, lanes):
+    row, lane = iota(0, (8, 128)), iota(1, (8, 128))
+    table = jnp.zeros((8, 128), F32)
+    target = jnp.full((8, 128), -1, jnp.int32)
+    for n, (part, at) in enumerate(zip(parts, lanes)):
+        table = jnp.where(row == n, jnp.sum(part, axis=0, keepdims=True), table)
+        target = jnp.where(row == n, at, target)
+    totals = jnp.sum(table, axis=1, keepdims=True)
+    return jnp.sum(jnp.where(lane == target, totals, 0.0), axis=0, keepdims=True)
 
 
 def send_kernel(b_ref, own_ref, left_ref, right_ref):
@@ -103,7 +114,7 @@
         out_ref[f, 1] = high_ref[SLAB_PLANE, :, :128]
 
 
-def curl_kernel(b_ref, low_ref, high_ref, u_ref, face_ref, t_ref, acc_ref):
+def curl_kernel(b_ref, low_ref, high_ref, u_ref, face_ref, t_ref, row_ref, keep_ref):
     st = Stencil()
     place = lax.axis_index("space")
     keep_next = jnp.where(place == N_SPACE - 1, 0.0, 1.0).astype(F32)
@@ -155,10 +166,8 @@
                     s3 = s3 + fold(total)
                 if i < PLANES:
                     u_old = (ux, uy, uz)
-        acc_ref[pol, 0] = s0
-        acc_ref[pol, 1] = s1
-        acc_ref[pol, 2] = s2
-        acc_ref[pol, 3] = s3
+        for n, value in enumerate((s0, s1, s2, s3)):
+            keep_ref[4 * pol + n] = value
         for i in range(PLANES):
             br = [b_ref[pol, 0, c, i] for c in range(3)]
             bi = [b_ref[pol, 1, c, i] for c in range(3)]
@@ -170,12 +179,13 @@
         return carry
 
     lax.fori_loop(0, 2, one_pol, 0)
-
-
-N_SUMS = 12
-
-
-def moment_kernel(got_ref, b_ref, high_ref, u_ref, face_ref, acc_ref, sigma_ref, sums_ref, next_ref):
+    row_ref[...] = placed([keep_ref[n] for n in range(8)], [n % 4 + 64 * (n // 4) for n in range(8)])
+
+
+N_SUMS = 10
+
+
+def moment_kernel(_, got_ref, b_ref, high_ref, u_ref, face_ref, row_ref, sigma_ref, sums_ref, next_ref, keep_ref):
     st = Stencil()
     is_first = jnp.where(lax.axis_index("space") == 0, 1.0, 0.0).astype(F32)
     group = iota(1, (DEPTH, 128)) // SLAB
@@ -193,10 +203,8 @@
             else:
                 next_ref[:, cols] = value
 
-    lane = iota(1, (1, 128))
-
-    def one_pol(pol, row):
-        names = ("d1", "d2", "d3", "e1", "e2", "g", "x1", "x2")
+    def one_pol(pol, carry):
+        names = ("d1", "d2", "d3", "e1", "re", "im")
         acc = {name: jnp.zeros((8, 128), F32) for name in names}
 
         def add(name, plane):
@@ -224,20 +232,20 @@
                 if i == 0:
                     x1 = x1 + is_first * (qy + qz)
                     x2 = x2 + is_first * (ry + rz)
-                add("x1", x1)
-                add("x2", x2)
                 add("d1", dot3(w, b))
                 add("d2", ww)
                 add("d3", s * ww)
                 add("e1", uw)
-                add("e2", s * dot3(u, u))
-                add("g", s * uw)
-        every = [acc_ref[pol, k] for k in range(4)] + [acc[name] for name in names]
-        for k, value in enumerate(every):
-            row = row + jnp.where(lane == k + 64 * pol, jnp.sum(value, axis=(0, 1), keepdims=True), 0.0)
-        return row
-
-    row = lax.fori_loop(0, 2, one_pol, jnp.zeros((1, 128), F32))
+                add("re", x2 + 2.0 * s * uw)
+                add("im", 2.0 * x1 + s * dot3(u, u))
+        for n, name in enumerate(names):
+            keep_ref[pol, n] = acc[name]
+        return carry
+
+    lax.fori_loop(0, 2, one_pol, 0)
+    row = row_ref[...]
+    for pol in range(2):
+        row = row + placed([keep_ref[pol, n] for n in range(6)], [64 * pol + 4 + n for n in range(6)])
     for k in range(N_SPACE):
         sums_ref[k] = row
 
@@ -255,14 +263,14 @@
     row = jnp.sum(jnp.concatenate([sums_ref[k] for k in range(N_SPACE)], axis=0), axis=0, keepdims=True)
     found = []
     for pol in range(2):
-        s0, s1, s2, s3, d1, d2, d3, e1, e2, g, x1, x2 = [
+        s0, s1, s2, s3, d1, d2, d3, e1, re, im = [
             row[:, k + 64 * pol : k + 64 * pol + 1] for k in range(N_SUMS)
         ]
         w2 = omega * omega
         m0 = (s0, jnp.zeros_like(s0))
         m1 = (s1, omega * d1)
         m2 = (s2 - w2 * d2, 2.0 * omega * e1)
-        m3 = (s3 - w2 * (2.0 * g + x2), omega * (2.0 * x1 + e2) - omega * w2 * d3)
+        m3 = (s3 - w2 * re, omega * im - omega * w2 * d3)
         a0 = over(m0, m1)
         a0a0 = times(a0, a0)
         z = times(a0a0, m2)
@@ -382,10 +390,11 @@
             shape(2, 2, 3, PLANES, DEPTH, WIDTH),
             shape(2, 2, 3, PLANES, DEPTH, WIDTH),
             shape(2, 3, PLANES, DEPTH, WIDTH),
-            shape(2, 4, 8, 128),
+            shape(1, 128),
         ),
         in_specs=[vmem()] * 3,
         out_specs=(vmem(),) * 4,
+        scratch_shapes=[pltpu.VMEM((8, 8, 128), F32)],
         compiler_params=params(),
         cost_estimate=cost(3.0),
         name="curl_curl",
@@ -393,13 +402,13 @@
     sigma, sums = pl.pallas_call(
         moment_kernel,
         out_shape=(shape(PLANES, DEPTH, WIDTH), shape(N_SPACE, 1, 128)),
-        in_specs=[vmem()] * 6,
+        in_specs=[smem()] + [vmem()] * 6,
         out_specs=(vmem(),) * 2,
-        scratch_shapes=[pltpu.VMEM((DEPTH, WIDTH), F32)],
+        scratch_shapes=[pltpu.VMEM((DEPTH, WIDTH), F32), pltpu.VMEM((2, 6, 8, 128), F32)],
         compiler_params=params(),
         cost_estimate=cost(2.0),
         name="moments",
-    )(got, b, high, u, faces, acc)
+    )(frequency, got, b, high, u, faces, acc)
     all_sums = lax.all_to_all(sums, "space", 0, 0)
     terms = pl.pallas_call(
         sense_kernel,

time: 57.4 us -> 56.5 us (0.984)
  blocking collectives: 0 us -> 17.5 us
  starting transfers between devices: 26.9 us -> 17.1 us
  waiting for transfers between devices: 18 us -> 10.1 us
  Pallas kernels: 7.5 us -> 6.79 us
    all_to_all x0 -> x1, blocking collectives: none -> 17.5 us  [local(): all_sums = lax.all_to_all(sums, 'space', 0, 0)]
    all_to_all x1 -> x0, starting transfers between devices: 9.85 us -> none  [local(): all_sums = lax.all_to_all(sums, 'space', 0, 0)]
    all_to_all x1 -> x0, waiting for transfers between devices: 7.13 us -> none  [local(): all_sums = lax.all_to_all(sums, 'space', 0, 0)]
    pallas_call x1, Pallas kernels: 1.65 us -> 0.86 us  [local(): pl.pallas_call(moment_kernel, out_shape=(shape(PLANES, DEPTH, WIDTH), sha...]
    ppermute x1, waiting for transfers between devices: 1.73 us -> 1.09 us  [local(): high = lax.ppermute(to_left, 'space', downward)]
  transfers between devices with their start and end apart: 5 -> 4, of which waited for: 4 -> 3; matrix products, arithmetic and copies ran while one was open for 1% -> 1% of each run, Pallas kernels for 6% -> 7%
where the time goes in v3:
time: 56.5 us; the launch traced here: 56 us
  blocking collectives  17.5 us (31%)
  starting transfers between devices  17.1 us (30%)
  waiting for transfers between devices  10.1 us (18%)
  Pallas kernels  6.79 us (12%)
  local copies, waits for them, and re-layouts  3.15 us (6%)
  between operations  1.36 us (2%)
    all_to_all x1, blocking collectives, local(): all_sums = lax.all_to_all(sums, 'space', 0, 0)  17.5 us
    all_to_all x1, starting transfers between devices, local(): got = lax.all_to_all(packed, 'freq', 0, 0)  6.53 us
    all_to_all x1, waiting for transfers between devices, local(): got = lax.all_to_all(packed, 'freq', 0, 0)  5.64 us
    ppermute x1, starting transfers between devices, local(): high = lax.ppermute(to_left, 'space', downward)  5.28 us
    all_to_all x1, waiting for transfers between devices, local(): shared = lax.all_to_all(terms, 'freq', 0, 0)  3.41 us
    all_to_all x1, starting transfers between devices, local(): shared = lax.all_to_all(terms, 'freq', 0, 0)  3.35 us
    unnamed x13, local copies, waits for them, and re-layouts  3.15 us
    ppermute x1, starting transfers between devices, local(): low = lax.ppermute(to_right, 'space', upward)  1.92 us
  transfers between devices with their start and end apart: 4, of which 3 were waited for; matrix products, arithmetic and copies ran while one was open for 1% of the time, Pallas kernels for 7%

profile of v3, /device:TPU:1, one launch (start us, length us, event | category | flops | bytes accessed | tf_op | source)
XLA Modules:
  0.0 56.0 jit_solution(11040596480901156866)
XLA Ops:
  0.6 0.0 copy-start
  0.6 1.1 %copy-done = f32[1,2,2,3,4,16,256]{6,5,4,3,2,1,0:T(8,128)S(1)} copy-done((f32[1,2,2,3,4,16,256]{6,5,4,3,2,1,0:T(8,128)S(1)}, f32[1,2,2,3,4,16,256]{6,5,4,3,2,1,0:T(8,128)}, u32[]{:S(2)}) %copy-start) | copy-done | bytes 786456
  1.8 0.0 copy-start.2
  1.8 0.8 %copy-done.2 = f32[4,16,32]{2,1,0:T(8,128)S(1)} copy-done((f32[4,16,32]{2,1,0:T(8,128)S(1)}, f32[4,16,32]{2,1,0:T(8,128)}, u32[]{:S(2)}) %copy-start.2) | copy-done | bytes 8216
  2.5 0.0 copy-start.1
  2.5 0.2 edge_planes.1
  2.7 5.3 %collective-permute-start = (f32[17,16,256]{2,1,0:T(8,128)S(1)}, f32[17,16,256]{2,1,0:T(8,128)S(1)}, u32[]{:S(2)}, u32[]{:S(2)}) collective-permute-start(f32[17,16,256]{2,1,0:T(8,128)S(1)} %get-tuple-element.13), channel_id=1, source_target_pairs={{1,0},{2,1},{3,2},{4,3},{5,4},{6,5},{7,6},{8,7},{9,8},{10,9},{11,1... | collective-permute-start | bytes 835592 | tf_op jit(solution)/shard_map/ppermute | solution.py:375
  8.0 1.9 %collective-permute-start.1 = (f32[8,16,256]{2,1,0:T(8,128)S(1)}, f32[8,16,256]{2,1,0:T(8,128)S(1)}, u32[]{:S(2)}, u32[]{:S(2)}) collective-permute-start(f32[8,16,256]{2,1,0:T(8,128)S(1)} %get-tuple-element.14), channel_id=1, source_target_pairs={{0,1},{1,2},{2,3},{3,4},{4,5},{5,6},{6,7},{7,8},{8,9},{9,10},{10,1... | collective-permute-start | bytes 393224 | tf_op jit(solution)/shard_map/ppermute | solution.py:376
  10.6 1.1 %collective-permute-done.high_ref = f32[17,16,256]{2,1,0:T(8,128)S(1)} collective-permute-done((f32[17,16,256]{2,1,0:T(8,128)S(1)}, f32[17,16,256]{2,1,0:T(8,128)S(1)}, u32[]{:S(2)}, u32[]{:S(2)}) %collective-permute-start) | collective-permute-done | bytes 278560 | tf_op jit(solution)/shard_map/ppermute | solution.py:375
  11.6 0.7 %pack_conductivity.1 = f32[8,2,16,128]{3,2,1,0:T(8,128)} custom-call(f32[4,16,32]{2,1,0:T(8,128)S(1)} %copy-done.2, f32[17,16,256]{2,1,0:T(8,128)S(1)} %collective-permute-done.high_ref), custom_call_target="tpu_custom_call" | custom-call | tf_op jit(solution)/shard_map/pack_conductivity/pallas_call | solution.py:377
  12.4 6.5 %all-to-all-start = ((f32[8,2,16,128]{3,2,1,0:T(8,128)}), f32[8,2,16,128]{3,2,1,0:T(8,128)S(1)}, u32[]{:S(2)}, u32[]{:S(2)}) async-start(f32[8,2,16,128]{3,2,1,0:T(8,128)} %pack_conductivity.1), calls=%async_computation | async-start | bytes 262144 | tf_op jit(solution)/shard_map/all_to_all | solution.py:385
  18.9 0.0 collective-permute-done.1.low_ref
  18.9 0.0 copy-done.1
  18.9 1.1 %curl_curl.1 = (f32[2,2,3,4,16,256]{5,4,3,2,1,0:T(8,128)S(1)}, f32[2,2,3,4,16,256]{5,4,3,2,1,0:T(8,128)S(1)}, f32[2,3,4,16,256]{4,3,2,1,0:T(8,128)S(1)}, f32[1,128]{1,0:T(1,128)S(1)}) custom-call(f32[2,2,3,4,16,256]{5,4,3,2,1,0:T(8,128)S(1)} %bitcast.6, f32[8,16,256]{2,1,0:T(8,128)S(1)} %collective-permute-done.1.low_ref, ...), custom_call_target="tpu_custom_call" | custom-call | flops 3000000000 | bytes 9000000 | tf_op jit(solution)/shard_map/curl_curl/pallas_call | solution.py:387
  20.0 5.6 %all-to-all-done.got_ref = f32[8,2,16,128]{3,2,1,0:T(8,128)S(1)} async-done(((f32[8,2,16,128]{3,2,1,0:T(8,128)}), f32[8,2,16,128]{3,2,1,0:T(8,128)S(1)}, u32[]{:S(2)}, u32[]{:S(2)}) %all-to-all-start) | async-done | bytes 131104 | tf_op jit(solution)/shard_map/all_to_all | solution.py:385
  25.7 0.9 %moments.1 = (f32[4,16,256]{2,1,0:T(8,128)S(1)}, f32[32,1,128]{2,1,0:T(1,128)S(1)}) custom-call(f32[1]{0:T(128)S(6)} %copy.9._.omega_ref, f32[8,2,16,128]{3,2,1,0:T(8,128)S(1)} %all-to-all-done.got_ref, f32[2,2,3,4,16,256]{5,4,3,2,1,0:T(8,128)S(1)} %bitcast.7, f32[17,16,256]{2,1,0:T(8,128)S(1)} %collective-permute-done.high_ref, ...), custom_call_target="tpu_custom_call" | custom-call | flops 2000000000 | bytes 6000000 | tf_op jit(solution)/shard_map/moments/pallas_call | solution.py:402
  26.5 17.5 %all_to_all.15.sums_ref = f32[32,1,128]{2,1,0:T(1,128)S(1)} all-to-all(f32[32,1,128]{2,1,0:T(1,128)S(1)} %get-tuple-element.18), channel_id=1, replica_groups=mesh['freq'=8,'space'=32] {'space'}, dimensions={0} | all-to-all | bytes 32768 | tf_op jit(solution)/shard_map/all_to_all | solution.py:412
  44.0 1.3 %sensitivity.1 = f32[8,16,128]{2,1,0:T(8,128)} custom-call(f32[1]{0:T(128)S(6)} %copy.9._.omega_ref, f32[32,1,128]{2,1,0:T(1,128)S(1)} %all_to_all.15.sums_ref, f32[2,3,4,16,256]{4,3,2,1,0:T(8,128)S(1)} %get-tuple-element.22.t_ref, f32[4,16,256]{2,1,0:T(8,128)S(1)} %get-tuple-element.19.sigma_ref), custom_call_target="tpu_custom_call" | custom-call | flops 1000000000 | bytes 3000000 | tf_op jit(solution)/shard_map/sensitivity/pallas_call | solution.py:413
  45.4 3.3 %all-to-all-start.2 = ((f32[8,16,128]{2,1,0:T(8,128)}), f32[8,16,128]{2,1,0:T(8,128)S(1)}, u32[]{:S(2)}, u32[]{:S(2)}) async-start(f32[8,16,128]{2,1,0:T(8,128)} %sensitivity.1), calls=%async_computation.2 | async-start | bytes 131072 | tf_op jit(solution)/shard_map/all_to_all | solution.py:422
  48.7 0.0 copy-start.4
  48.7 0.0 copy-start.5
  48.7 0.6 %copy-done.4 = s32[64]{0:T(128)S(1)} copy-done((s32[64]{0:T(128)S(1)}, s32[64]{0:T(128)}, u32[]{:S(2)}) %copy-start.4) | copy-done | bytes 280
  49.4 0.0 copy-done.5
  49.4 0.0 copy-start.3
  49.4 1.9 %field.1 = (f32[2,2,3,4,16,256]{5,4,3,2,1,0:T(8,128)}, f32[2,2,3,64]{3,2,1,0:T(4,128)S(1)}) custom-call(f32[1]{0:T(128)S(6)} %copy.9._.omega_ref, f32[32,1,128]{2,1,0:T(1,128)S(1)} %all_to_all.15.sums_ref, f32[2,2,3,4,16,256]{5,4,3,2,1,0:T(8,128)S(1)} %bitcast.8, f32[2,2,3,4,16,256]{5,4,3,2,1,0:T(8,128)S(1)} %get-tuple-element.15.u_ref, ...), custom_call_target="tpu_custom_call" | custom-call | flops 3000000000 | bytes 9000000 | tf_op jit(solution)/shard_map/field/pallas_call | solution.py:423
  51.3 0.6 %copy.8 = f32[1,2,2,3,64]{4,2,3,1,0:T(2,128)} copy(f32[1,2,2,3,64]{4,3,2,1,0:T(4,128)S(1)} %bitcast.9) | data formatting | bytes 6144
  51.9 3.4 %all-to-all-done.2.terms_ref = f32[8,16,128]{2,1,0:T(8,128)S(1)} async-done(((f32[8,16,128]{2,1,0:T(8,128)}), f32[8,16,128]{2,1,0:T(8,128)S(1)}, u32[]{:S(2)}, u32[]{:S(2)}) %all-to-all-start.2) | async-done | bytes 65568 | tf_op jit(solution)/shard_map/all_to_all | solution.py:422
  55.3 0.0 copy-done.3
  55.3 0.7 %gradient.1 = f32[4,16,32]{2,1,0:T(8,128)} custom-call(f32[8,16,128]{2,1,0:T(8,128)S(1)} %all-to-all-done.2.terms_ref, f32[4,16,32]{2,1,0:T(8,128)S(1)} %copy-done.3), custom_call_target="tpu_custom_call" | custom-call | tf_op jit(solution)/shard_map/gradient/pallas_call | solution.py:432
Async XLA Ops:
  0.6 1.1 %copy-start = (f32[1,2,2,3,4,16,256]{6,5,4,3,2,1,0:T(8,128)S(1)}, f32[1,2,2,3,4,16,256]{6,5,4,3,2,1,0:T(8,128)}, u32[]{:S(2)}) copy-start(f32[1,2,2,3,4,16,256]{6,5,4,3,2,1,0:T(8,128)} %param.5) | copy-start | bytes 2359300
  1.8 0.8 %copy-start.2 = (f32[4,16,32]{2,1,0:T(8,128)S(1)}, f32[4,16,32]{2,1,0:T(8,128)}, u32[]{:S(2)}) copy-start(f32[4,16,32]{2,1,0:T(8,128)} %own_ref.5) | copy-start | bytes 24580
  2.5 16.4 %copy-start.1 = (f32[1,2,2,3,4,16,256]{6,5,4,3,2,1,0:T(8,128)S(1)}, f32[1,2,2,3,4,16,256]{6,5,4,3,2,1,0:T(8,128)}, u32[]{:S(2)}) copy-start(f32[1,2,2,3,4,16,256]{6,5,4,3,2,1,0:T(8,128)} %param.5) | copy-start | bytes 2359300
  2.7 9.0 %collective-permute-start = (f32[17,16,256]{2,1,0:T(8,128)S(1)}, f32[17,16,256]{2,1,0:T(8,128)S(1)}, u32[]{:S(2)}, u32[]{:S(2)}) collective-permute-start(f32[17,16,256]{2,1,0:T(8,128)S(1)} %get-tuple-element.13), channel_id=1, source_target_pairs={{1,0},{2,1},{3,2},{4,3},{5,4},{6,5},{7,6},{8,7},{9,8},{10,9},{11,1... | collective-permute-start | bytes 835592 | tf_op jit(solution)/shard_map/ppermute | solution.py:375
  8.0 10.9 %collective-permute-start.1 = (f32[8,16,256]{2,1,0:T(8,128)S(1)}, f32[8,16,256]{2,1,0:T(8,128)S(1)}, u32[]{:S(2)}, u32[]{:S(2)}) collective-permute-start(f32[8,16,256]{2,1,0:T(8,128)S(1)} %get-tuple-element.14), channel_id=1, source_target_pairs={{0,1},{1,2},{2,3},{3,4},{4,5},{5,6},{6,7},{7,8},{8,9},{9,10},{10,1... | collective-permute-start | bytes 393224 | tf_op jit(solution)/shard_map/ppermute | solution.py:376
  12.4 13.3 %all-to-all-start = ((f32[8,2,16,128]{3,2,1,0:T(8,128)}), f32[8,2,16,128]{3,2,1,0:T(8,128)S(1)}, u32[]{:S(2)}, u32[]{:S(2)}) async-start(f32[8,2,16,128]{3,2,1,0:T(8,128)} %pack_conductivity.1), calls=%async_computation | async-start | bytes 262144 | tf_op jit(solution)/shard_map/all_to_all | solution.py:385
  45.4 10.0 %all-to-all-start.2 = ((f32[8,16,128]{2,1,0:T(8,128)}), f32[8,16,128]{2,1,0:T(8,128)S(1)}, u32[]{:S(2)}, u32[]{:S(2)}) async-start(f32[8,16,128]{2,1,0:T(8,128)} %sensitivity.1), calls=%async_computation.2 | async-start | bytes 131072 | tf_op jit(solution)/shard_map/all_to_all | solution.py:422
  48.7 0.7 %copy-start.4 = (s32[64]{0:T(128)S(1)}, s32[64]{0:T(128)}, u32[]{:S(2)}) copy-start(s32[64]{0:T(128)} %param.8) | copy-start | bytes 772
  48.7 0.7 %copy-start.5 = (s32[64]{0:T(128)S(1)}, s32[64]{0:T(128)}, u32[]{:S(2)}) copy-start(s32[64]{0:T(128)} %param.9) | copy-start | bytes 772
  49.4 5.9 %copy-start.3 = (f32[4,16,32]{2,1,0:T(8,128)S(1)}, f32[4,16,32]{2,1,0:T(8,128)}, u32[]{:S(2)}) copy-start(f32[4,16,32]{2,1,0:T(8,128)} %own_ref.5) | copy-start | bytes 24580

commit v4 on v3

--- a/solution.py
+++ b/solution.py
@@ -88,19 +88,29 @@
     return jnp.sum(jnp.where(lane == target, totals, 0.0), axis=0, keepdims=True)
 
 
-def send_kernel(b_ref, own_ref, left_ref, right_ref):
+def send_kernel(b_ref, sigma_ref, left_ref, right_ref, front_ref, second_ref, last_ref, own_ref, sems):
+    copies = [
+        pltpu.make_async_copy(b_ref.at[:, :, :, 0], front_ref, sems.at[0]),
+        pltpu.make_async_copy(b_ref.at[:, :, pl.ds(1, 2), 1], second_ref, sems.at[1]),
+        pltpu.make_async_copy(b_ref.at[:, :, :, LAST], last_ref, sems.at[2]),
+        pltpu.make_async_copy(sigma_ref.at[pl.ds(0, 1)], own_ref, sems.at[3]),
+    ]
+    for copy in copies:
+        copy.start()
+    for copy in copies:
+        copy.wait()
     st = Stencil()
     for pol in range(2):
         for part in range(2):
             k = 2 * pol + part
-            ex, ey, ez = [b_ref[pol, part, c, 0] for c in range(3)]
+            ex, ey, ez = [front_ref[pol, part, c] for c in range(3)]
             hx = st.face_x(ey, ez)
-            hy, hz = st.faces_yz(ex, ey, ez, b_ref[pol, part, 1, 1], b_ref[pol, part, 2, 1])
+            hy, hz = st.faces_yz(ex, ey, ez, second_ref[pol, part, 0], second_ref[pol, part, 1])
             left_ref[4 * k] = ey
             left_ref[4 * k + 1] = ez
             left_ref[4 * k + 2] = st.bz(hx, -ey) - hz
             left_ref[4 * k + 3] = hy - st.by(hx, ez)
-            ex, ey, ez = [b_ref[pol, part, c, LAST] for c in range(3)]
+            ex, ey, ez = [last_ref[pol, part, c] for c in range(3)]
             right_ref[2 * k] = st.fz(ex) + ez
             right_ref[2 * k + 1] = -ey - st.fy(ex)
     front = jnp.concatenate([own_ref[0]] * 4, axis=1)
@@ -260,31 +270,32 @@
 
 
 def steps(sums_ref, omega):
-    row = jnp.sum(jnp.concatenate([sums_ref[k] for k in range(N_SPACE)], axis=0), axis=0, keepdims=True)
+    row = jnp.sum(sums_ref[...], axis=0)
     found = []
     for pol in range(2):
         s0, s1, s2, s3, d1, d2, d3, e1, re, im = [
-            row[:, k + 64 * pol : k + 64 * pol + 1] for k in range(N_SUMS)
+            jnp.broadcast_to(row[:, k + 64 * pol : k + 64 * pol + 1], (1, 128)) for k in range(N_SUMS)
         ]
         w2 = omega * omega
-        m0 = (s0, jnp.zeros_like(s0))
-        m1 = (s1, omega * d1)
-        m2 = (s2 - w2 * d2, 2.0 * omega * e1)
-        m3 = (s3 - w2 * re, omega * im - omega * w2 * d3)
-        a0 = over(m0, m1)
+        scale = 1.0 / s0
+        n1 = (s1, omega * d1)
+        n2 = (s2 - w2 * d2, 2.0 * omega * e1)
+        n3 = (s3 - w2 * re, omega * im - omega * w2 * d3)
+        inverse = s0 / (n1[0] * n1[0] + n1[1] * n1[1])
+        a0 = (n1[0] * inverse, -n1[1] * inverse)
         a0a0 = times(a0, a0)
-        z = times(a0a0, m2)
+        z = times(a0a0, n2)
         rho = (z[0] - s0, z[1])
-        grow = (1.0 + rho[0] / s0, rho[1] / s0)
-        first = times(times(grow, grow), m1)
-        second = times(times(a0, grow), m2)
-        third = times(a0a0, m3)
+        grow = (1.0 + rho[0] * scale, rho[1] * scale)
+        first = times(times(grow, grow), n1)
+        second = times(times(a0, grow), n2)
+        third = times(a0a0, n3)
         curv = (first[0] - 2.0 * second[0] + third[0], first[1] - 2.0 * second[1] + third[1])
         a1 = over(rho, curv)
         a1g = times(a1, grow)
         a1a0 = times(a1, a0)
         found.append(((a0[0] + a1g[0], a0[1] + a1g[1]), (-a1a0[0], -a1a0[1])))
-    return found
+    return [tuple((jnp.concatenate([r, r], axis=1), jnp.concatenate([i, i], axis=1)) for r, i in pair) for pair in found]
 
 
 def sense_kernel(omega_ref, sums_ref, t_ref, sigma_ref, out_ref):
@@ -367,11 +378,18 @@
     to_left, to_right = pl.pallas_call(
         send_kernel,
         out_shape=(shape(SLAB_PLANE + 1, DEPTH, WIDTH), shape(8, DEPTH, WIDTH)),
-        in_specs=[vmem(), vmem()],
+        in_specs=[pl.BlockSpec(memory_space=pltpu.HBM)] * 2,
         out_specs=(vmem(), vmem()),
+        scratch_shapes=[
+            pltpu.VMEM((2, 2, 3, DEPTH, WIDTH), F32),
+            pltpu.VMEM((2, 2, 2, DEPTH, WIDTH), F32),
+            pltpu.VMEM((2, 2, 3, DEPTH, WIDTH), F32),
+            pltpu.VMEM((1, DEPTH, SLAB), F32),
+            pltpu.SemaphoreType.DMA((4,)),
+        ],
         compiler_params=params(),
         name="edge_planes",
-    )(b, conductivity)
+    )(pltpu.with_memory_space_constraint(b, pltpu.HBM), pltpu.with_memory_space_constraint(conductivity, pltpu.HBM))
     high = lax.ppermute(to_left, "space", downward)
     low = lax.ppermute(to_right, "space", upward)
     packed = pl.pallas_call(

time: 56.5 us -> 55.2 us (0.977)
  local copies, waits for them, and re-layouts: 3.15 us -> 1.26 us
    unnamed x13 -> x9, local copies, waits for them, and re-layouts: 3.15 us -> 1.26 us
    pallas_call x1, Pallas kernels: 0.16 us -> 1.37 us  [local(): pl.pallas_call(send_kernel, out_shape=(shape(SLAB_PLANE + 1, DEPTH, WIDTH...]
  transfers between devices with their start and end apart: 4 -> 4, of which waited for: 3 -> 3; matrix products, arithmetic and copies ran while one was open for 1% -> 1% of each run, Pallas kernels for 7% -> 6%
where the time goes in v4:
time: 55.2 us; the launch traced here: 54.8 us
  blocking collectives  17.5 us (32%)
  starting transfers between devices  16.9 us (31%)
  waiting for transfers between devices  10.4 us (19%)
  Pallas kernels  7.34 us (13%)
  between operations  1.36 us (2%)
  local copies, waits for them, and re-layouts  1.26 us (2%)
    all_to_all x1, blocking collectives, local(): all_sums = lax.all_to_all(sums, 'space', 0, 0)  17.5 us
    all_to_all x1, starting transfers between devices, local(): got = lax.all_to_all(packed, 'freq', 0, 0)  6.53 us
    all_to_all x1, waiting for transfers between devices, local(): got = lax.all_to_all(packed, 'freq', 0, 0)  5.64 us
    ppermute x1, starting transfers between devices, local(): high = lax.ppermute(to_left, 'space', downward)  5.15 us
    all_to_all x1, waiting for transfers between devices, local(): shared = lax.all_to_all(terms, 'freq', 0, 0)  3.68 us
    all_to_all x1, starting transfers between devices, local(): shared = lax.all_to_all(terms, 'freq', 0, 0)  3.35 us
    ppermute x1, starting transfers between devices, local(): low = lax.ppermute(to_right, 'space', upward)  1.92 us
    pallas_call x1, Pallas kernels, local(): pl.pallas_call(field_kernel, out_shape=(shape(2, 2, 3, PLANES, DEPTH, WID...  1.65 us
  transfers between devices with their start and end apart: 4, of which 3 were waited for; matrix products, arithmetic and copies ran while one was open for 1% of the time, Pallas kernels for 6%

profile of v4, /device:TPU:1, one launch (start us, length us, event | category | flops | bytes accessed | tf_op | source)
XLA Modules:
  0.0 54.8 jit_solution(8901347855659730552)
XLA Ops:
  0.6 0.0 copy-start
  0.6 0.0 copy-start.1
  0.6 1.4 %edge_planes.1 = (f32[17,16,256]{2,1,0:T(8,128)S(1)}, f32[8,16,256]{2,1,0:T(8,128)S(1)}) custom-call(f32[2,2,3,4,16,256]{5,4,3,2,1,0:T(8,128)} %bitcast.5, f32[4,16,32]{2,1,0:T(8,128)} %own_ref.3), custom_call_target="tpu_custom_call" | custom-call | tf_op jit(solution)/shard_map/edge_planes/pallas_call | solution.py:378
  2.0 5.1 %collective-permute-start = (f32[17,16,256]{2,1,0:T(8,128)S(1)}, f32[17,16,256]{2,1,0:T(8,128)S(1)}, u32[]{:S(2)}, u32[]{:S(2)}) collective-permute-start(f32[17,16,256]{2,1,0:T(8,128)S(1)} %get-tuple-element.13), channel_id=1, source_target_pairs={{1,0},{2,1},{3,2},{4,3},{5,4},{6,5},{7,6},{8,7},{9,8},{10,9},{11,1... | collective-permute-start | bytes 835592 | tf_op jit(solution)/shard_map/ppermute | solution.py:393
  7.2 1.9 %collective-permute-start.1 = (f32[8,16,256]{2,1,0:T(8,128)S(1)}, f32[8,16,256]{2,1,0:T(8,128)S(1)}, u32[]{:S(2)}, u32[]{:S(2)}) collective-permute-start(f32[8,16,256]{2,1,0:T(8,128)S(1)} %get-tuple-element.14), channel_id=1, source_target_pairs={{0,1},{1,2},{2,3},{3,4},{4,5},{5,6},{6,7},{7,8},{8,9},{9,10},{10,1... | collective-permute-start | bytes 393224 | tf_op jit(solution)/shard_map/ppermute | solution.py:394
  9.8 1.1 %collective-permute-done.high_ref = f32[17,16,256]{2,1,0:T(8,128)S(1)} collective-permute-done((f32[17,16,256]{2,1,0:T(8,128)S(1)}, f32[17,16,256]{2,1,0:T(8,128)S(1)}, u32[]{:S(2)}, u32[]{:S(2)}) %collective-permute-start) | collective-permute-done | bytes 278560 | tf_op jit(solution)/shard_map/ppermute | solution.py:393
  10.8 0.0 copy-done.1
  10.8 0.7 %pack_conductivity.1 = f32[8,2,16,128]{3,2,1,0:T(8,128)} custom-call(f32[4,16,32]{2,1,0:T(8,128)S(1)} %copy-done.1, f32[17,16,256]{2,1,0:T(8,128)S(1)} %collective-permute-done.high_ref), custom_call_target="tpu_custom_call" | custom-call | tf_op jit(solution)/shard_map/pack_conductivity/pallas_call | solution.py:395
  11.6 6.5 %all-to-all-start = ((f32[8,2,16,128]{3,2,1,0:T(8,128)}), f32[8,2,16,128]{3,2,1,0:T(8,128)S(1)}, u32[]{:S(2)}, u32[]{:S(2)}) async-start(f32[8,2,16,128]{3,2,1,0:T(8,128)} %pack_conductivity.1), calls=%async_computation | async-start | bytes 262144 | tf_op jit(solution)/shard_map/all_to_all | solution.py:403
  18.1 0.0 collective-permute-done.1.low_ref
  18.1 0.0 copy-done
  18.1 1.1 %curl_curl.1 = (f32[2,2,3,4,16,256]{5,4,3,2,1,0:T(8,128)S(1)}, f32[2,2,3,4,16,256]{5,4,3,2,1,0:T(8,128)S(1)}, f32[2,3,4,16,256]{4,3,2,1,0:T(8,128)S(1)}, f32[1,128]{1,0:T(1,128)S(1)}) custom-call(f32[2,2,3,4,16,256]{5,4,3,2,1,0:T(8,128)S(1)} %bitcast.6, f32[8,16,256]{2,1,0:T(8,128)S(1)} %collective-permute-done.1.low_ref, ...), custom_call_target="tpu_custom_call" | custom-call | flops 3000000000 | bytes 9000000 | tf_op jit(solution)/shard_map/curl_curl/pallas_call | solution.py:405
  19.2 5.6 %all-to-all-done.got_ref = f32[8,2,16,128]{3,2,1,0:T(8,128)S(1)} async-done(((f32[8,2,16,128]{3,2,1,0:T(8,128)}), f32[8,2,16,128]{3,2,1,0:T(8,128)S(1)}, u32[]{:S(2)}, u32[]{:S(2)}) %all-to-all-start) | async-done | bytes 131104 | tf_op jit(solution)/shard_map/all_to_all | solution.py:403
  24.9 0.9 %moments.1 = (f32[4,16,256]{2,1,0:T(8,128)S(1)}, f32[32,1,128]{2,1,0:T(1,128)S(1)}) custom-call(f32[1]{0:T(128)S(6)} %copy.9._.omega_ref, f32[8,2,16,128]{3,2,1,0:T(8,128)S(1)} %all-to-all-done.got_ref, f32[2,2,3,4,16,256]{5,4,3,2,1,0:T(8,128)S(1)} %bitcast.7, f32[17,16,256]{2,1,0:T(8,128)S(1)} %collective-permute-done.high_ref, ...), custom_call_target="tpu_custom_call" | custom-call | flops 2000000000 | bytes 6000000 | tf_op jit(solution)/shard_map/moments/pallas_call | solution.py:420
  25.7 17.5 %all_to_all.15.sums_ref = f32[32,1,128]{2,1,0:T(1,128)S(1)} all-to-all(f32[32,1,128]{2,1,0:T(1,128)S(1)} %get-tuple-element.18), channel_id=1, replica_groups=mesh['freq'=8,'space'=32] {'space'}, dimensions={0} | all-to-all | bytes 32768 | tf_op jit(solution)/shard_map/all_to_all | solution.py:430
  43.2 0.9 %sensitivity.1 = f32[8,16,128]{2,1,0:T(8,128)} custom-call(f32[1]{0:T(128)S(6)} %copy.9._.omega_ref, f32[32,1,128]{2,1,0:T(1,128)S(1)} %all_to_all.15.sums_ref, f32[2,3,4,16,256]{4,3,2,1,0:T(8,128)S(1)} %get-tuple-element.22.t_ref, f32[4,16,256]{2,1,0:T(8,128)S(1)} %get-tuple-element.19.sigma_ref), custom_call_target="tpu_custom_call" | custom-call | flops 1000000000 | bytes 3000000 | tf_op jit(solution)/shard_map/sensitivity/pallas_call | solution.py:431
  44.2 3.3 %all-to-all-start.2 = ((f32[8,16,128]{2,1,0:T(8,128)}), f32[8,16,128]{2,1,0:T(8,128)S(1)}, u32[]{:S(2)}, u32[]{:S(2)}) async-start(f32[8,16,128]{2,1,0:T(8,128)} %sensitivity.1), calls=%async_computation.2 | async-start | bytes 131072 | tf_op jit(solution)/shard_map/all_to_all | solution.py:440
  47.5 0.0 copy-start.2
  47.5 0.0 copy-start.3
  47.5 0.6 %copy-done.2 = s32[64]{0:T(128)S(1)} copy-done((s32[64]{0:T(128)S(1)}, s32[64]{0:T(128)}, u32[]{:S(2)}) %copy-start.2) | copy-done | bytes 280
  48.2 0.0 copy-done.3
  48.2 1.6 %field.1 = (f32[2,2,3,4,16,256]{5,4,3,2,1,0:T(8,128)}, f32[2,2,3,64]{3,2,1,0:T(4,128)S(1)}) custom-call(f32[1]{0:T(128)S(6)} %copy.9._.omega_ref, f32[32,1,128]{2,1,0:T(1,128)S(1)} %all_to_all.15.sums_ref, f32[2,2,3,4,16,256]{5,4,3,2,1,0:T(8,128)S(1)} %bitcast.8, f32[2,2,3,4,16,256]{5,4,3,2,1,0:T(8,128)S(1)} %get-tuple-element.15.u_ref, ...), custom_call_target="tpu_custom_call" | custom-call | flops 3000000000 | bytes 9000000 | tf_op jit(solution)/shard_map/field/pallas_call | solution.py:441
  49.8 0.6 %copy.8 = f32[1,2,2,3,64]{4,2,3,1,0:T(2,128)} copy(f32[1,2,2,3,64]{4,3,2,1,0:T(4,128)S(1)} %bitcast.9) | data formatting | bytes 6144
  50.4 3.7 %all-to-all-done.2.terms_ref = f32[8,16,128]{2,1,0:T(8,128)S(1)} async-done(((f32[8,16,128]{2,1,0:T(8,128)}), f32[8,16,128]{2,1,0:T(8,128)S(1)}, u32[]{:S(2)}, u32[]{:S(2)}) %all-to-all-start.2) | async-done | bytes 65568 | tf_op jit(solution)/shard_map/all_to_all | solution.py:440
  54.1 0.7 %gradient.1 = f32[4,16,32]{2,1,0:T(8,128)} custom-call(f32[8,16,128]{2,1,0:T(8,128)S(1)} %all-to-all-done.2.terms_ref, f32[4,16,32]{2,1,0:T(8,128)S(1)} %copy-done.1), custom_call_target="tpu_custom_call" | custom-call | tf_op jit(solution)/shard_map/gradient/pallas_call | solution.py:450
Async XLA Ops:
  0.6 17.5 %copy-start = (f32[1,2,2,3,4,16,256]{6,5,4,3,2,1,0:T(8,128)S(1)}, f32[1,2,2,3,4,16,256]{6,5,4,3,2,1,0:T(8,128)}, u32[]{:S(2)}) copy-start(f32[1,2,2,3,4,16,256]{6,5,4,3,2,1,0:T(8,128)} %param.5) | copy-start | bytes 2359300
  0.6 10.2 %copy-start.1 = (f32[4,16,32]{2,1,0:T(8,128)S(1)}, f32[4,16,32]{2,1,0:T(8,128)}, u32[]{:S(2)}) copy-start(f32[4,16,32]{2,1,0:T(8,128)} %own_ref.3) | copy-start | bytes 24580
  2.0 8.8 %collective-permute-start = (f32[17,16,256]{2,1,0:T(8,128)S(1)}, f32[17,16,256]{2,1,0:T(8,128)S(1)}, u32[]{:S(2)}, u32[]{:S(2)}) collective-permute-start(f32[17,16,256]{2,1,0:T(8,128)S(1)} %get-tuple-element.13), channel_id=1, source_target_pairs={{1,0},{2,1},{3,2},{4,3},{5,4},{6,5},{7,6},{8,7},{9,8},{10,9},{11,1... | collective-permute-start | bytes 835592 | tf_op jit(solution)/shard_map/ppermute | solution.py:393
  7.2 10.9 %collective-permute-start.1 = (f32[8,16,256]{2,1,0:T(8,128)S(1)}, f32[8,16,256]{2,1,0:T(8,128)S(1)}, u32[]{:S(2)}, u32[]{:S(2)}) collective-permute-start(f32[8,16,256]{2,1,0:T(8,128)S(1)} %get-tuple-element.14), channel_id=1, source_target_pairs={{0,1},{1,2},{2,3},{3,4},{4,5},{5,6},{6,7},{7,8},{8,9},{9,10},{10,1... | collective-permute-start | bytes 393224 | tf_op jit(solution)/shard_map/ppermute | solution.py:394
  11.6 13.3 %all-to-all-start = ((f32[8,2,16,128]{3,2,1,0:T(8,128)}), f32[8,2,16,128]{3,2,1,0:T(8,128)S(1)}, u32[]{:S(2)}, u32[]{:S(2)}) async-start(f32[8,2,16,128]{3,2,1,0:T(8,128)} %pack_conductivity.1), calls=%async_computation | async-start | bytes 262144 | tf_op jit(solution)/shard_map/all_to_all | solution.py:403
  44.2 10.0 %all-to-all-start.2 = ((f32[8,16,128]{2,1,0:T(8,128)}), f32[8,16,128]{2,1,0:T(8,128)S(1)}, u32[]{:S(2)}, u32[]{:S(2)}) async-start(f32[8,16,128]{2,1,0:T(8,128)} %sensitivity.1), calls=%async_computation.2 | async-start | bytes 131072 | tf_op jit(solution)/shard_map/all_to_all | solution.py:440
  47.5 0.7 %copy-start.2 = (s32[64]{0:T(128)S(1)}, s32[64]{0:T(128)}, u32[]{:S(2)}) copy-start(s32[64]{0:T(128)} %param.8) | copy-start | bytes 772
  47.5 0.7 %copy-start.3 = (s32[64]{0:T(128)S(1)}, s32[64]{0:T(128)}, u32[]{:S(2)}) copy-start(s32[64]{0:T(128)} %param.9) | copy-start | bytes 772

commit v5 on v4

--- a/solution.py
+++ b/solution.py
@@ -9,6 +9,8 @@
 F32 = jnp.float32
 N_FREQ = 8
 N_SPACE = 32
+FREQ_ORDER = list(range(N_FREQ))[::-1]
+SPACE_ORDER = [(i + 16) % N_SPACE for i in range(N_SPACE)]
 DEPTH = 16
 WIDTH = 256
 PLANES = 4
@@ -204,7 +206,7 @@
         for i in range(PLANES + 1):
             value = None
             for q in range(4):
-                piece = got_ref[4 * half + q, 0 if i < PLANES else 1]
+                piece = got_ref[FREQ_ORDER[4 * half + q], 0 if i < PLANES else 1]
                 shift = (SLAB * (q - i)) % 128 if i < PLANES else 0
                 piece = pltpu.roll(piece, shift, 1) if shift else piece
                 value = piece if value is None else jnp.where(group == q, piece, value)
@@ -322,7 +324,7 @@
             shift = (SLAB * (i - q)) % 128
             piece = pltpu.roll(piece, shift, 1) if shift else piece
             value = piece if value is None else jnp.where(group == i, piece, value)
-        out_ref[f] = value
+        out_ref[FREQ_ORDER[f]] = value
 
 
 def field_kernel(omega_ref, sums_ref, b_ref, u_ref, sigma_ref, cells_ref, depth_ref, x_ref, sampled_ref):
@@ -400,7 +402,7 @@
         compiler_params=params(),
         name="pack_conductivity",
     )(conductivity, high)
-    got = lax.all_to_all(packed, "freq", 0, 0)
+    got = lax.all_to_all(packed, "freq", 0, 0, axis_index_groups=[FREQ_ORDER])
 
     u, faces, products, acc = pl.pallas_call(
         curl_kernel,
@@ -427,7 +429,7 @@
         cost_estimate=cost(2.0),
         name="moments",
     )(frequency, got, b, high, u, faces, acc)
-    all_sums = lax.all_to_all(sums, "space", 0, 0)
+    all_sums = lax.all_to_all(sums, "space", 0, 0, axis_index_groups=[SPACE_ORDER])
     terms = pl.pallas_call(
         sense_kernel,
         out_shape=shape(N_FREQ, DEPTH, 128),
@@ -437,7 +439,7 @@
         cost_estimate=cost(1.0),
         name="sensitivity",
     )(frequency, all_sums, products, sigma)
-    shared = lax.all_to_all(terms, "freq", 0, 0)
+    shared = lax.all_to_all(terms, "freq", 0, 0, axis_index_groups=[FREQ_ORDER])
     x, sampled = pl.pallas_call(
         field_kernel,
         out_shape=(shape(2, 2, 3, PLANES, DEPTH, WIDTH), shape(2, 2, 3, stations)),

time: 55.2 us -> 50.1 us (0.908)
  waiting for transfers between devices: 10.4 us -> 3.03 us
  starting transfers between devices: 16.9 us -> 22.4 us
  blocking collectives: 17.5 us -> 14.3 us
    all_to_all x2, waiting for transfers between devices: 9.32 us -> 1.94 us  [the longest x1 1.9 us: local(): got = lax.all_to_all(packed, 'freq', 0, 0, axis_index_groups=[FREQ_ORDER])]
    all_to_all x2, starting transfers between devices: 9.88 us -> 15.3 us  [the longest x1 8.3 us: local(): got = lax.all_to_all(packed, 'freq', 0, 0, axis_index_groups=[FREQ_ORDER])]
    all_to_all x1, blocking collectives: 17.5 us -> 14.3 us  [local(): lax.all_to_all(sums, 'space', 0, 0, axis_index_groups=[SPACE_ORDER])]
  transfers between devices with their start and end apart: 4 -> 4, of which waited for: 3 -> 2; matrix products, arithmetic and copies ran while one was open for 1% -> 1% of each run, Pallas kernels for 6% -> 7%
where the time goes in v5:
time: 50.1 us; the launch traced here: 49.7 us
  starting transfers between devices  22.4 us (45%)
  blocking collectives  14.3 us (29%)
  Pallas kernels  7.34 us (15%)
  waiting for transfers between devices  3.03 us (6%)
  between operations  1.34 us (3%)
  local copies, waits for them, and re-layouts  1.27 us (3%)
    all_to_all x1, blocking collectives, local(): lax.all_to_all(sums, 'space', 0, 0, axis_index_groups=[SPACE_ORDER])  14.3 us
    all_to_all x1, starting transfers between devices, local(): got = lax.all_to_all(packed, 'freq', 0, 0, axis_index_groups=[FREQ_ORDER])  8.3 us
    all_to_all x1, starting transfers between devices, local(): shared = lax.all_to_all(terms, 'freq', 0, 0, axis_index_groups=[FREQ_ORDER])  7.03 us
    ppermute x1, starting transfers between devices, local(): high = lax.ppermute(to_left, 'space', downward)  5.15 us
    ppermute x1, starting transfers between devices, local(): low = lax.ppermute(to_right, 'space', upward)  1.92 us
    all_to_all x1, waiting for transfers between devices, local(): got = lax.all_to_all(packed, 'freq', 0, 0, axis_index_groups=[FREQ_ORDER])  1.9 us
    pallas_call x1, Pallas kernels, local(): pl.pallas_call(field_kernel, out_shape=(shape(2, 2, 3, PLANES, DEPTH, WID...  1.65 us
    pallas_call x1, Pallas kernels, local(): pl.pallas_call(send_kernel, out_shape=(shape(SLAB_PLANE + 1, DEPTH, WIDTH...  1.37 us
  transfers between devices with their start and end apart: 4, of which 2 were waited for; matrix products, arithmetic and copies ran while one was open for 1% of the time, Pallas kernels for 7%

profile of v5, /device:TPU:1, one launch (start us, length us, event | category | flops | bytes accessed | tf_op | source)
XLA Modules:
  0.0 49.7 jit_solution(720584706774660895)
XLA Ops:
  0.6 0.0 copy-start
  0.6 0.0 copy-start.1
  0.6 1.4 %edge_planes.1 = (f32[17,16,256]{2,1,0:T(8,128)S(1)}, f32[8,16,256]{2,1,0:T(8,128)S(1)}) custom-call(f32[2,2,3,4,16,256]{5,4,3,2,1,0:T(8,128)} %bitcast.5, f32[4,16,32]{2,1,0:T(8,128)} %own_ref.3), custom_call_target="tpu_custom_call" | custom-call | tf_op jit(solution)/shard_map/edge_planes/pallas_call | solution.py:380
  2.0 5.1 %collective-permute-start = (f32[17,16,256]{2,1,0:T(8,128)S(1)}, f32[17,16,256]{2,1,0:T(8,128)S(1)}, u32[]{:S(2)}, u32[]{:S(2)}) collective-permute-start(f32[17,16,256]{2,1,0:T(8,128)S(1)} %get-tuple-element.13), channel_id=1, source_target_pairs={{1,0},{2,1},{3,2},{4,3},{5,4},{6,5},{7,6},{8,7},{9,8},{10,9},{11,1... | collective-permute-start | bytes 835592 | tf_op jit(solution)/shard_map/ppermute | solution.py:395
  7.2 1.9 %collective-permute-start.1 = (f32[8,16,256]{2,1,0:T(8,128)S(1)}, f32[8,16,256]{2,1,0:T(8,128)S(1)}, u32[]{:S(2)}, u32[]{:S(2)}) collective-permute-start(f32[8,16,256]{2,1,0:T(8,128)S(1)} %get-tuple-element.14), channel_id=1, source_target_pairs={{0,1},{1,2},{2,3},{3,4},{4,5},{5,6},{6,7},{7,8},{8,9},{9,10},{10,1... | collective-permute-start | bytes 393224 | tf_op jit(solution)/shard_map/ppermute | solution.py:396
  9.8 1.1 %collective-permute-done.high_ref = f32[17,16,256]{2,1,0:T(8,128)S(1)} collective-permute-done((f32[17,16,256]{2,1,0:T(8,128)S(1)}, f32[17,16,256]{2,1,0:T(8,128)S(1)}, u32[]{:S(2)}, u32[]{:S(2)}) %collective-permute-start) | collective-permute-done | bytes 278560 | tf_op jit(solution)/shard_map/ppermute | solution.py:395
  10.8 0.0 copy-done.1
  10.8 0.7 %pack_conductivity.1 = f32[8,2,16,128]{3,2,1,0:T(8,128)} custom-call(f32[4,16,32]{2,1,0:T(8,128)S(1)} %copy-done.1, f32[17,16,256]{2,1,0:T(8,128)S(1)} %collective-permute-done.high_ref), custom_call_target="tpu_custom_call" | custom-call | tf_op jit(solution)/shard_map/pack_conductivity/pallas_call | solution.py:397
  11.6 8.3 %all-to-all-start = ((f32[8,2,16,128]{3,2,1,0:T(8,128)}), f32[8,2,16,128]{3,2,1,0:T(8,128)S(1)}, u32[]{:S(2)}, u32[]{:S(2)}) async-start(f32[8,2,16,128]{3,2,1,0:T(8,128)} %pack_conductivity.1), calls=%async_computation | async-start | bytes 262144 | tf_op jit(solution)/shard_map/all_to_all | solution.py:405
  19.9 0.0 collective-permute-done.1.low_ref
  19.9 0.0 copy-done
  19.9 1.1 %curl_curl.1 = (f32[2,2,3,4,16,256]{5,4,3,2,1,0:T(8,128)S(1)}, f32[2,2,3,4,16,256]{5,4,3,2,1,0:T(8,128)S(1)}, f32[2,3,4,16,256]{4,3,2,1,0:T(8,128)S(1)}, f32[1,128]{1,0:T(1,128)S(1)}) custom-call(f32[2,2,3,4,16,256]{5,4,3,2,1,0:T(8,128)S(1)} %bitcast.6, f32[8,16,256]{2,1,0:T(8,128)S(1)} %collective-permute-done.1.low_ref, ...), custom_call_target="tpu_custom_call" | custom-call | flops 3000000000 | bytes 9000000 | tf_op jit(solution)/shard_map/curl_curl/pallas_call | solution.py:407
  21.0 1.9 %all-to-all-done.got_ref = f32[8,2,16,128]{3,2,1,0:T(8,128)S(1)} async-done(((f32[8,2,16,128]{3,2,1,0:T(8,128)}), f32[8,2,16,128]{3,2,1,0:T(8,128)S(1)}, u32[]{:S(2)}, u32[]{:S(2)}) %all-to-all-start) | async-done | bytes 131104 | tf_op jit(solution)/shard_map/all_to_all | solution.py:405
  22.9 0.9 %moments.1 = (f32[4,16,256]{2,1,0:T(8,128)S(1)}, f32[32,1,128]{2,1,0:T(1,128)S(1)}) custom-call(f32[1]{0:T(128)S(6)} %copy.9._.omega_ref, f32[8,2,16,128]{3,2,1,0:T(8,128)S(1)} %all-to-all-done.got_ref, f32[2,2,3,4,16,256]{5,4,3,2,1,0:T(8,128)S(1)} %bitcast.7, f32[17,16,256]{2,1,0:T(8,128)S(1)} %collective-permute-done.high_ref, ...), custom_call_target="tpu_custom_call" | custom-call | flops 2000000000 | bytes 6000000 | tf_op jit(solution)/shard_map/moments/pallas_call | solution.py:422
  23.8 14.3 %all_to_all.15.sums_ref = f32[32,1,128]{2,1,0:T(1,128)S(1)} all-to-all(f32[32,1,128]{2,1,0:T(1,128)S(1)} %get-tuple-element.18), channel_id=1, replica_groups={{16,17,18,19,20,21,22,23,24,25,26,27,28,29,30,31,0,1,2,3,4,5,6,7,8,9,10..., dimensions={0} | all-to-all | bytes 32768 | tf_op jit(solution)/shard_map/all_to_all | solution.py:432
  38.1 0.9 %sensitivity.1 = f32[8,16,128]{2,1,0:T(8,128)} custom-call(f32[1]{0:T(128)S(6)} %copy.9._.omega_ref, f32[32,1,128]{2,1,0:T(1,128)S(1)} %all_to_all.15.sums_ref, f32[2,3,4,16,256]{4,3,2,1,0:T(8,128)S(1)} %get-tuple-element.22.t_ref, f32[4,16,256]{2,1,0:T(8,128)S(1)} %get-tuple-element.19.sigma_ref), custom_call_target="tpu_custom_call" | custom-call | flops 1000000000 | bytes 3000000 | tf_op jit(solution)/shard_map/sensitivity/pallas_call | solution.py:433
  39.0 7.0 %all-to-all-start.2 = ((f32[8,16,128]{2,1,0:T(8,128)}), f32[8,16,128]{2,1,0:T(8,128)S(1)}, u32[]{:S(2)}, u32[]{:S(2)}) async-start(f32[8,16,128]{2,1,0:T(8,128)} %sensitivity.1), calls=%async_computation.2 | async-start | bytes 131072 | tf_op jit(solution)/shard_map/all_to_all | solution.py:442
  46.0 0.0 copy-start.2
  46.0 0.0 copy-start.3
  46.0 0.7 %copy-done.2 = s32[64]{0:T(128)S(1)} copy-done((s32[64]{0:T(128)S(1)}, s32[64]{0:T(128)}, u32[]{:S(2)}) %copy-start.2) | copy-done | bytes 280
  46.7 0.0 copy-done.3
  46.7 1.6 %field.1 = (f32[2,2,3,4,16,256]{5,4,3,2,1,0:T(8,128)}, f32[2,2,3,64]{3,2,1,0:T(4,128)S(1)}) custom-call(f32[1]{0:T(128)S(6)} %copy.9._.omega_ref, f32[32,1,128]{2,1,0:T(1,128)S(1)} %all_to_all.15.sums_ref, f32[2,2,3,4,16,256]{5,4,3,2,1,0:T(8,128)S(1)} %bitcast.8, f32[2,2,3,4,16,256]{5,4,3,2,1,0:T(8,128)S(1)} %get-tuple-element.15.u_ref, ...), custom_call_target="tpu_custom_call" | custom-call | flops 3000000000 | bytes 9000000 | tf_op jit(solution)/shard_map/field/pallas_call | solution.py:443
  48.3 0.6 %copy.8 = f32[1,2,2,3,64]{4,2,3,1,0:T(2,128)} copy(f32[1,2,2,3,64]{4,3,2,1,0:T(4,128)S(1)} %bitcast.9) | data formatting | bytes 6144
  48.9 0.0 all-to-all-done.2.terms_ref
  49.0 0.7 %gradient.1 = f32[4,16,32]{2,1,0:T(8,128)} custom-call(f32[8,16,128]{2,1,0:T(8,128)S(1)} %all-to-all-done.2.terms_ref, f32[4,16,32]{2,1,0:T(8,128)S(1)} %copy-done.1), custom_call_target="tpu_custom_call" | custom-call | tf_op jit(solution)/shard_map/gradient/pallas_call | solution.py:452
Async XLA Ops:
  0.6 19.3 %copy-start = (f32[1,2,2,3,4,16,256]{6,5,4,3,2,1,0:T(8,128)S(1)}, f32[1,2,2,3,4,16,256]{6,5,4,3,2,1,0:T(8,128)}, u32[]{:S(2)}) copy-start(f32[1,2,2,3,4,16,256]{6,5,4,3,2,1,0:T(8,128)} %param.5) | copy-start | bytes 2359300
  0.6 10.2 %copy-start.1 = (f32[4,16,32]{2,1,0:T(8,128)S(1)}, f32[4,16,32]{2,1,0:T(8,128)}, u32[]{:S(2)}) copy-start(f32[4,16,32]{2,1,0:T(8,128)} %own_ref.3) | copy-start | bytes 24580
  2.0 8.8 %collective-permute-start = (f32[17,16,256]{2,1,0:T(8,128)S(1)}, f32[17,16,256]{2,1,0:T(8,128)S(1)}, u32[]{:S(2)}, u32[]{:S(2)}) collective-permute-start(f32[17,16,256]{2,1,0:T(8,128)S(1)} %get-tuple-element.13), channel_id=1, source_target_pairs={{1,0},{2,1},{3,2},{4,3},{5,4},{6,5},{7,6},{8,7},{9,8},{10,9},{11,1... | collective-permute-start | bytes 835592 | tf_op jit(solution)/shard_map/ppermute | solution.py:395
  7.2 12.7 %collective-permute-start.1 = (f32[8,16,256]{2,1,0:T(8,128)S(1)}, f32[8,16,256]{2,1,0:T(8,128)S(1)}, u32[]{:S(2)}, u32[]{:S(2)}) collective-permute-start(f32[8,16,256]{2,1,0:T(8,128)S(1)} %get-tuple-element.14), channel_id=1, source_target_pairs={{0,1},{1,2},{2,3},{3,4},{4,5},{5,6},{6,7},{7,8},{8,9},{9,10},{10,1... | collective-permute-start | bytes 393224 | tf_op jit(solution)/shard_map/ppermute | solution.py:396
  11.6 11.3 %all-to-all-start = ((f32[8,2,16,128]{3,2,1,0:T(8,128)}), f32[8,2,16,128]{3,2,1,0:T(8,128)S(1)}, u32[]{:S(2)}, u32[]{:S(2)}) async-start(f32[8,2,16,128]{3,2,1,0:T(8,128)} %pack_conductivity.1), calls=%async_computation | async-start | bytes 262144 | tf_op jit(solution)/shard_map/all_to_all | solution.py:405
  39.0 10.0 %all-to-all-start.2 = ((f32[8,16,128]{2,1,0:T(8,128)}), f32[8,16,128]{2,1,0:T(8,128)S(1)}, u32[]{:S(2)}, u32[]{:S(2)}) async-start(f32[8,16,128]{2,1,0:T(8,128)} %sensitivity.1), calls=%async_computation.2 | async-start | bytes 131072 | tf_op jit(solution)/shard_map/all_to_all | solution.py:442
  46.0 0.7 %copy-start.2 = (s32[64]{0:T(128)S(1)}, s32[64]{0:T(128)}, u32[]{:S(2)}) copy-start(s32[64]{0:T(128)} %param.8) | copy-start | bytes 772
  46.0 0.7 %copy-start.3 = (s32[64]{0:T(128)S(1)}, s32[64]{0:T(128)}, u32[]{:S(2)}) copy-start(s32[64]{0:T(128)} %param.9) | copy-start | bytes 772

commit v6 on v5

--- a/solution.py
+++ b/solution.py
@@ -10,7 +10,7 @@
 N_FREQ = 8
 N_SPACE = 32
 FREQ_ORDER = list(range(N_FREQ))[::-1]
-SPACE_ORDER = [(i + 16) % N_SPACE for i in range(N_SPACE)]
+SPACE_ORDER = [(19 - i) % N_SPACE for i in range(N_SPACE)]
 DEPTH = 16
 WIDTH = 256
 PLANES = 4
@@ -26,8 +26,8 @@
     return pl.BlockSpec(memory_space=pltpu.VMEM)
 
 
-def anywhere():
-    return pl.BlockSpec(memory_space=pl.ANY)
+def hbm():
+    return pl.BlockSpec(memory_space=pltpu.HBM)
 
 
 def smem():
@@ -119,14 +119,20 @@
     left_ref[SLAB_PLANE] = jnp.concatenate([front, front], axis=1)
 
 
-def pack_kernel(own_ref, high_ref, out_ref):
-    own = jnp.concatenate([own_ref[i] for i in range(PLANES)], axis=1)
-    for f in range(N_FREQ):
-        out_ref[f, 0] = own
-        out_ref[f, 1] = high_ref[SLAB_PLANE, :, :128]
-
-
-def curl_kernel(b_ref, low_ref, high_ref, u_ref, face_ref, t_ref, row_ref, keep_ref):
+def pack_kernel(own_ref, high_ref, out_ref, both_ref, sems):
+    both_ref[0] = jnp.concatenate([own_ref[i] for i in range(PLANES)], axis=1)
+    both_ref[1] = high_ref[SLAB_PLANE, :, :128]
+    copies = [pltpu.make_async_copy(both_ref, out_ref.at[f], sems.at[f]) for f in range(N_FREQ)]
+    for copy in copies:
+        copy.start()
+    for copy in copies:
+        copy.wait()
+
+
+def curl_kernel(source_ref, low_ref, high_ref, b_ref, u_ref, face_ref, t_ref, row_ref, keep_ref, sem):
+    load = pltpu.make_async_copy(source_ref, b_ref, sem)
+    load.start()
+    load.wait()
     st = Stencil()
     place = lax.axis_index("space")
     keep_next = jnp.where(place == N_SPACE - 1, 0.0, 1.0).astype(F32)
@@ -372,6 +378,7 @@
 
 def local(source_current, conductivity, frequency, station_cells, station_depth):
     b = source_current[0]
+    b_far = pltpu.with_memory_space_constraint(b, pltpu.HBM)
     stations = station_cells.shape[0]
     ends = N_SPACE - 1
     upward = [(i, i + 1) for i in range(ends)]
@@ -380,7 +387,7 @@
     to_left, to_right = pl.pallas_call(
         send_kernel,
         out_shape=(shape(SLAB_PLANE + 1, DEPTH, WIDTH), shape(8, DEPTH, WIDTH)),
-        in_specs=[pl.BlockSpec(memory_space=pltpu.HBM)] * 2,
+        in_specs=[hbm()] * 2,
         out_specs=(vmem(), vmem()),
         scratch_shapes=[
             pltpu.VMEM((2, 2, 3, DEPTH, WIDTH), F32),
@@ -391,34 +398,36 @@
         ],
         compiler_params=params(),
         name="edge_planes",
-    )(pltpu.with_memory_space_constraint(b, pltpu.HBM), pltpu.with_memory_space_constraint(conductivity, pltpu.HBM))
+    )(b_far, pltpu.with_memory_space_constraint(conductivity, pltpu.HBM))
     high = lax.ppermute(to_left, "space", downward)
     low = lax.ppermute(to_right, "space", upward)
     packed = pl.pallas_call(
         pack_kernel,
-        out_shape=shape(N_FREQ, 2, DEPTH, 128),
+        out_shape=pltpu.HBM((N_FREQ, 2, DEPTH, 128), F32),
         in_specs=[vmem(), vmem()],
-        out_specs=vmem(),
+        out_specs=hbm(),
+        scratch_shapes=[pltpu.VMEM((2, DEPTH, 128), F32), pltpu.SemaphoreType.DMA((N_FREQ,))],
         compiler_params=params(),
         name="pack_conductivity",
     )(conductivity, high)
     got = lax.all_to_all(packed, "freq", 0, 0, axis_index_groups=[FREQ_ORDER])
 
-    u, faces, products, acc = pl.pallas_call(
+    held, u, faces, products, acc = pl.pallas_call(
         curl_kernel,
         out_shape=(
+            shape(2, 2, 3, PLANES, DEPTH, WIDTH),
             shape(2, 2, 3, PLANES, DEPTH, WIDTH),
             shape(2, 2, 3, PLANES, DEPTH, WIDTH),
             shape(2, 3, PLANES, DEPTH, WIDTH),
             shape(1, 128),
         ),
-        in_specs=[vmem()] * 3,
-        out_specs=(vmem(),) * 4,
-        scratch_shapes=[pltpu.VMEM((8, 8, 128), F32)],
+        in_specs=[hbm()] + [vmem()] * 2,
+        out_specs=(vmem(),) * 5,
+        scratch_shapes=[pltpu.VMEM((8, 8, 128), F32), pltpu.SemaphoreType.DMA],
         compiler_params=params(),
         cost_estimate=cost(3.0),
         name="curl_curl",
-    )(b, low, high)
+    )(b_far, low, high)
     sigma, sums = pl.pallas_call(
         moment_kernel,
         out_shape=(shape(PLANES, DEPTH, WIDTH), shape(N_SPACE, 1, 128)),
@@ -428,7 +437,7 @@
         compiler_params=params(),
         cost_estimate=cost(2.0),
         name="moments",
-    )(frequency, got, b, high, u, faces, acc)
+    )(frequency, got, held, high, u, faces, acc)
     all_sums = lax.all_to_all(sums, "space", 0, 0, axis_index_groups=[SPACE_ORDER])
     terms = pl.pallas_call(
         sense_kernel,
@@ -448,7 +457,7 @@
         compiler_params=params(),
         cost_estimate=cost(3.0),
         name="field",
-    )(frequency, all_sums, b, u, sigma, station_cells[None], station_depth[None])
+    )(frequency, all_sums, held, u, sigma, station_cells[None], station_depth[None])
     gradient = pl.pallas_call(
         gradient_kernel,
         out_shape=shape(PLANES, DEPTH, SLAB),

time: 50.1 us -> 49.8 us (level)
  waiting for transfers between devices: 3.03 us -> 1.89 us
  Pallas kernels: 7.34 us -> 8.46 us
    all_to_all x1, waiting for transfers between devices: 1.9 us -> 0.76 us  [local(): got = lax.all_to_all(packed, 'freq', 0, 0, axis_index_groups=[FREQ_ORDER])]
    pallas_call x1, Pallas kernels: 1.11 us -> 2.24 us  [local(): pl.pallas_call(curl_kernel, out_shape=(shape(2, 2, 3, PLANES, DEPTH, WIDT...]
    unnamed x9 -> x7, local copies, waits for them, and re-layouts: 1.27 us -> 1.27 us
  transfers between devices with their start and end apart: 4 -> 4, of which waited for: 2 -> 2; matrix products, arithmetic and copies ran while one was open for 1% -> 1% of each run, Pallas kernels for 7% -> 9%
where the time goes in v6:
time: 49.8 us; the launch traced here: 49.3 us
  starting transfers between devices  22.3 us (45%)
  blocking collectives  14 us (28%)
  Pallas kernels  8.46 us (17%)
  waiting for transfers between devices  1.89 us (4%)
  between operations  1.34 us (3%)
  local copies, waits for them, and re-layouts  1.27 us (3%)
    all_to_all x1, blocking collectives, local(): lax.all_to_all(sums, 'space', 0, 0, axis_index_groups=[SPACE_ORDER])  14 us
    all_to_all x1, starting transfers between devices, local(): got = lax.all_to_all(packed, 'freq', 0, 0, axis_index_groups=[FREQ_ORDER])  8.31 us
    all_to_all x1, starting transfers between devices, local(): shared = lax.all_to_all(terms, 'freq', 0, 0, axis_index_groups=[FREQ_ORDER])  6.92 us
    ppermute x1, starting transfers between devices, local(): high = lax.ppermute(to_left, 'space', downward)  5.15 us
    pallas_call x1, Pallas kernels, local(): pl.pallas_call(curl_kernel, out_shape=(shape(2, 2, 3, PLANES, DEPTH, WIDT...  2.24 us
    ppermute x1, starting transfers between devices, local(): low = lax.ppermute(to_right, 'space', upward)  1.92 us
    pallas_call x1, Pallas kernels, local(): pl.pallas_call(field_kernel, out_shape=(shape(2, 2, 3, PLANES, DEPTH, WID...  1.65 us
    pallas_call x1, Pallas kernels, local(): pl.pallas_call(send_kernel, out_shape=(shape(SLAB_PLANE + 1, DEPTH, WIDTH...  1.3 us
  transfers between devices with their start and end apart: 4, of which 2 were waited for; matrix products, arithmetic and copies ran while one was open for 1% of the time, Pallas kernels for 9%

profile of v6, /device:TPU:1, one launch (start us, length us, event | category | flops | bytes accessed | tf_op | source)
XLA Modules:
  0.0 49.3 jit_solution(17188478956181184765)
XLA Ops:
  0.6 0.0 copy-start
  0.6 1.3 %edge_planes.1 = (f32[17,16,256]{2,1,0:T(8,128)S(1)}, f32[8,16,256]{2,1,0:T(8,128)S(1)}) custom-call(f32[2,2,3,4,16,256]{5,4,3,2,1,0:T(8,128)} %bitcast.8, f32[4,16,32]{2,1,0:T(8,128)} %own_ref.3), custom_call_target="tpu_custom_call" | custom-call | tf_op jit(solution)/shard_map/edge_planes/pallas_call | solution.py:387
  1.9 5.1 %collective-permute-start = (f32[17,16,256]{2,1,0:T(8,128)S(1)}, f32[17,16,256]{2,1,0:T(8,128)S(1)}, u32[]{:S(2)}, u32[]{:S(2)}) collective-permute-start(f32[17,16,256]{2,1,0:T(8,128)S(1)} %get-tuple-element.14), channel_id=1, source_target_pairs={{1,0},{2,1},{3,2},{4,3},{5,4},{6,5},{7,6},{8,7},{9,8},{10,9},{11,1... | collective-permute-start | bytes 835592 | tf_op jit(solution)/shard_map/ppermute | solution.py:402
  7.1 1.9 %collective-permute-start.1 = (f32[8,16,256]{2,1,0:T(8,128)S(1)}, f32[8,16,256]{2,1,0:T(8,128)S(1)}, u32[]{:S(2)}, u32[]{:S(2)}) collective-permute-start(f32[8,16,256]{2,1,0:T(8,128)S(1)} %get-tuple-element.15), channel_id=1, source_target_pairs={{0,1},{1,2},{2,3},{3,4},{4,5},{5,6},{6,7},{7,8},{8,9},{9,10},{10,1... | collective-permute-start | bytes 393224 | tf_op jit(solution)/shard_map/ppermute | solution.py:403
  9.7 1.1 %collective-permute-done.high_ref = f32[17,16,256]{2,1,0:T(8,128)S(1)} collective-permute-done((f32[17,16,256]{2,1,0:T(8,128)S(1)}, f32[17,16,256]{2,1,0:T(8,128)S(1)}, u32[]{:S(2)}, u32[]{:S(2)}) %collective-permute-start) | collective-permute-done | bytes 278560 | tf_op jit(solution)/shard_map/ppermute | solution.py:402
  10.8 0.0 copy-done
  10.8 0.8 %pack_conductivity.1 = f32[8,2,16,128]{3,2,1,0:T(8,128)} custom-call(f32[4,16,32]{2,1,0:T(8,128)S(1)} %copy-done, f32[17,16,256]{2,1,0:T(8,128)S(1)} %collective-permute-done.high_ref), custom_call_target="tpu_custom_call" | custom-call | tf_op jit(solution)/shard_map/pack_conductivity/pallas_call | solution.py:404
  11.6 8.3 %all-to-all-start = ((f32[8,2,16,128]{3,2,1,0:T(8,128)}), f32[8,2,16,128]{3,2,1,0:T(8,128)S(1)}, u32[]{:S(2)}, u32[]{:S(2)}) async-start(f32[8,2,16,128]{3,2,1,0:T(8,128)} %pack_conductivity.1), calls=%async_computation | async-start | bytes 262144 | tf_op jit(solution)/shard_map/all_to_all | solution.py:413
  19.9 0.0 collective-permute-done.1.low_ref
  19.9 2.2 %curl_curl.1 = (f32[2,2,3,4,16,256]{5,4,3,2,1,0:T(8,128)S(1)}, f32[2,2,3,4,16,256]{5,4,3,2,1,0:T(8,128)S(1)}, f32[2,2,3,4,16,256]{5,4,3,2,1,0:T(8,128)S(1)}, f32...) custom-call(f32[2,2,3,4,16,256]{5,4,3,2,1,0:T(8,128)} %bitcast.9, f32[8,16,256]{2,1,0:T(8,128)S(1)} %collective-permute-done.1.low_ref, ...), custom_call_target="tpu_custom_call" | custom-call | flops 3000000000 | bytes 9000000 | tf_op jit(solution)/shard_map/curl_curl/pallas_call | solution.py:415
  22.1 0.8 %all-to-all-done.got_ref = f32[8,2,16,128]{3,2,1,0:T(8,128)S(1)} async-done(((f32[8,2,16,128]{3,2,1,0:T(8,128)}), f32[8,2,16,128]{3,2,1,0:T(8,128)S(1)}, u32[]{:S(2)}, u32[]{:S(2)}) %all-to-all-start) | async-done | bytes 131104 | tf_op jit(solution)/shard_map/all_to_all | solution.py:413
  22.9 0.9 %moments.1 = (f32[4,16,256]{2,1,0:T(8,128)S(1)}, f32[32,1,128]{2,1,0:T(1,128)S(1)}) custom-call(f32[1]{0:T(128)S(6)} %copy.9._.omega_ref, f32[8,2,16,128]{3,2,1,0:T(8,128)S(1)} %all-to-all-done.got_ref, f32[2,2,3,4,16,256]{5,4,3,2,1,0:T(8,128)S(1)} %get-tuple-element.16.b_ref, f32[17,16,256]{2,1,0:T(8,128)S(1)} %collective-permute-done.high_ref, ...), custom_call_target="tpu_custom_call" | custom-call | flops 2000000000 | bytes 6000000 | tf_op jit(solution)/shard_map/moments/pallas_call | solution.py:431
  23.8 14.0 %all_to_all.15.sums_ref = f32[32,1,128]{2,1,0:T(1,128)S(1)} all-to-all(f32[32,1,128]{2,1,0:T(1,128)S(1)} %get-tuple-element.20), channel_id=1, replica_groups={{19,18,17,16,15,14,13,12,11,10,9,8,7,6,5,4,3,2,1,0,31,30,29,28,27,26,25..., dimensions={0} | all-to-all | bytes 32768 | tf_op jit(solution)/shard_map/all_to_all | solution.py:441
  37.8 0.9 %sensitivity.1 = f32[8,16,128]{2,1,0:T(8,128)} custom-call(f32[1]{0:T(128)S(6)} %copy.9._.omega_ref, f32[32,1,128]{2,1,0:T(1,128)S(1)} %all_to_all.15.sums_ref, f32[2,3,4,16,256]{4,3,2,1,0:T(8,128)S(1)} %get-tuple-element.24.t_ref, f32[4,16,256]{2,1,0:T(8,128)S(1)} %get-tuple-element.21.sigma_ref), custom_call_target="tpu_custom_call" | custom-call | flops 1000000000 | bytes 3000000 | tf_op jit(solution)/shard_map/sensitivity/pallas_call | solution.py:442
  38.7 6.9 %all-to-all-start.2 = ((f32[8,16,128]{2,1,0:T(8,128)}), f32[8,16,128]{2,1,0:T(8,128)S(1)}, u32[]{:S(2)}, u32[]{:S(2)}) async-start(f32[8,16,128]{2,1,0:T(8,128)} %sensitivity.1), calls=%async_computation.2 | async-start | bytes 131072 | tf_op jit(solution)/shard_map/all_to_all | solution.py:451
  45.7 0.0 copy-start.1
  45.7 0.0 copy-start.2
  45.7 0.7 %copy-done.1 = s32[64]{0:T(128)S(1)} copy-done((s32[64]{0:T(128)S(1)}, s32[64]{0:T(128)}, u32[]{:S(2)}) %copy-start.1) | copy-done | bytes 280
  46.3 0.0 copy-done.2
  46.3 1.6 %field.1 = (f32[2,2,3,4,16,256]{5,4,3,2,1,0:T(8,128)}, f32[2,2,3,64]{3,2,1,0:T(4,128)S(1)}) custom-call(f32[1]{0:T(128)S(6)} %copy.9._.omega_ref, f32[32,1,128]{2,1,0:T(1,128)S(1)} %all_to_all.15.sums_ref, f32[2,2,3,4,16,256]{5,4,3,2,1,0:T(8,128)S(1)} %get-tuple-element.16.b_ref, f32[2,2,3,4,16,256]{5,4,3,2,1,0:T(8,128)S(1)} %get-tuple-element.17.u_ref, ...), custom_call_target="tpu_custom_call" | custom-call | flops 3000000000 | bytes 9000000 | tf_op jit(solution)/shard_map/field/pallas_call | solution.py:452
  48.0 0.6 %copy.8 = f32[1,2,2,3,64]{4,2,3,1,0:T(2,128)} copy(f32[1,2,2,3,64]{4,3,2,1,0:T(4,128)S(1)} %bitcast.5) | data formatting | bytes 6144
  48.6 0.0 all-to-all-done.2.terms_ref
  48.6 0.7 %gradient.1 = f32[4,16,32]{2,1,0:T(8,128)} custom-call(f32[8,16,128]{2,1,0:T(8,128)S(1)} %all-to-all-done.2.terms_ref, f32[4,16,32]{2,1,0:T(8,128)S(1)} %copy-done), custom_call_target="tpu_custom_call" | custom-call | tf_op jit(solution)/shard_map/gradient/pallas_call | solution.py:461
Async XLA Ops:
  0.6 10.1 %copy-start = (f32[4,16,32]{2,1,0:T(8,128)S(1)}, f32[4,16,32]{2,1,0:T(8,128)}, u32[]{:S(2)}) copy-start(f32[4,16,32]{2,1,0:T(8,128)} %own_ref.3) | copy-start | bytes 24580
  1.9 8.8 %collective-permute-start = (f32[17,16,256]{2,1,0:T(8,128)S(1)}, f32[17,16,256]{2,1,0:T(8,128)S(1)}, u32[]{:S(2)}, u32[]{:S(2)}) collective-permute-start(f32[17,16,256]{2,1,0:T(8,128)S(1)} %get-tuple-element.14), channel_id=1, source_target_pairs={{1,0},{2,1},{3,2},{4,3},{5,4},{6,5},{7,6},{8,7},{9,8},{10,9},{11,1... | collective-permute-start | bytes 835592 | tf_op jit(solution)/shard_map/ppermute | solution.py:402
  7.1 12.8 %collective-permute-start.1 = (f32[8,16,256]{2,1,0:T(8,128)S(1)}, f32[8,16,256]{2,1,0:T(8,128)S(1)}, u32[]{:S(2)}, u32[]{:S(2)}) collective-permute-start(f32[8,16,256]{2,1,0:T(8,128)S(1)} %get-tuple-element.15), channel_id=1, source_target_pairs={{0,1},{1,2},{2,3},{3,4},{4,5},{5,6},{6,7},{7,8},{8,9},{9,10},{10,1... | collective-permute-start | bytes 393224 | tf_op jit(solution)/shard_map/ppermute | solution.py:403
  11.6 11.3 %all-to-all-start = ((f32[8,2,16,128]{3,2,1,0:T(8,128)}), f32[8,2,16,128]{3,2,1,0:T(8,128)S(1)}, u32[]{:S(2)}, u32[]{:S(2)}) async-start(f32[8,2,16,128]{3,2,1,0:T(8,128)} %pack_conductivity.1), calls=%async_computation | async-start | bytes 262144 | tf_op jit(solution)/shard_map/all_to_all | solution.py:413
  38.7 9.9 %all-to-all-start.2 = ((f32[8,16,128]{2,1,0:T(8,128)}), f32[8,16,128]{2,1,0:T(8,128)S(1)}, u32[]{:S(2)}, u32[]{:S(2)}) async-start(f32[8,16,128]{2,1,0:T(8,128)} %sensitivity.1), calls=%async_computation.2 | async-start | bytes 131072 | tf_op jit(solution)/shard_map/all_to_all | solution.py:451
  45.7 0.7 %copy-start.1 = (s32[64]{0:T(128)S(1)}, s32[64]{0:T(128)}, u32[]{:S(2)}) copy-start(s32[64]{0:T(128)} %param.8) | copy-start | bytes 772
  45.7 0.7 %copy-start.2 = (s32[64]{0:T(128)S(1)}, s32[64]{0:T(128)}, u32[]{:S(2)}) copy-start(s32[64]{0:T(128)} %param.9) | copy-start | bytes 772
